TPU v7x, 32 devices: a whole 2x2x4 slice. The times are simulated.
32 devices in a mesh: dom: 32 (over z, y, x, core).
Axes of the slice: x: 2, y: 2, z: 4, core: 2. Of those that a mesh axis runs over, the one named last changes fastest.
Arguments:
- features: bfloat16 [32768, 768], P('dom'), may hold values from -6 to 6
- w_self: bfloat16 [768, 1024], replicated, may hold values from -0.21875 to 0.21875
- w_neigh: bfloat16 [768, 1024], replicated, may hold values from -0.875 to 0.875
- cotangent: bfloat16 [32768, 1024], P('dom'), may hold values from -6 to 6
- tiles: bfloat16 [256, 8, 128, 128], P('dom'), may hold values from 0 to 1, as said below
- tile_src: int32 [256, 8], P('dom'), may hold values from 0 to 12, as said below
- tile_count: int32 [256], P('dom'), may hold values from 1 to 8
- send_rows: int32 [32, 32, 16], P('dom'), may hold values from 0 to 1023
- send_count: int32 [32, 32], P('dom'), may hold values from 0 to 16, as said below
- hub_rows: int32 [32, 4], P('dom'), may hold values from 0 to 1023
Outputs:
- layer_out: bfloat16 [32768, 1024], P('dom')
- grad_features: float32 [32768, 768], P('dom')
- grad_w_self: float32 [768, 1024], P('dom')
- grad_w_neigh: float32 [768, 1024], P('dom')
Inputs may be any that keep to these rules, and one draw needn't show every extreme that they name: `tile_src`: slot 0 of each block names the block itself (block t mod 1024/128 of the own rows); other slots name any block of the source table. `send_count`: A partition sends nothing to itself. `tiles`: Nonnegative; slot 0 of every block has a positive diagonal.
All inputs are finite; a program needn't handle non-finite values.
Results may differ from a plain program's by a relative error of at most 0.0052.
Values may be sent and summed in bfloat16 or wider, within the bound.
No kernel may reach another device: no remote copies, remote signals or barrier semaphores. Data moves between devices by JAX's collectives and lax.ppermute only.
A program may use at most 128 MiB of HBM per device.

v0:
```python
import jax
import jax.numpy as jnp
from jax import lax
from jax.sharding import PartitionSpec as P


def on_device(
    features,
    w_self,
    w_neigh,
    cotangent,
    tiles,
    tile_src,
    tile_count,
    send_rows,
    send_count,
    hub_rows,
):
    groups = lax.axis_size("dom")
    position = lax.axis_index("dom")
    own_rows, width = features.shape
    blocks_own, slots, tile_rows, _ = tiles.shape
    cap_rows = send_rows.shape[2]
    hub_own = hub_rows.shape[1]
    bnd_rows = groups * cap_rows
    hub_total = groups * hub_own
    sources = (own_rows + bnd_rows + hub_total) // tile_rows
    rows_out = send_rows[0]
    counts_out = send_count[0]
    slot_range = jnp.arange(cap_rows, dtype=jnp.int32)
    out_valid = slot_range[None, :] < counts_out[:, None]
    outgoing = jnp.where(out_valid[:, :, None], features[rows_out], jnp.zeros((), jnp.bfloat16))
    boundary, counts_in = (
        lax.all_to_all(outgoing, "dom", split_axis=0, concat_axis=0, tiled=True),
        lax.all_to_all(counts_out[:, None], "dom", split_axis=0, concat_axis=0, tiled=True),
    )
    in_valid = (slot_range[None, :] < counts_in).astype(jnp.float32).reshape(bnd_rows)
    boundary = boundary.reshape(bnd_rows, width)
    hub_mine = features[hub_rows[0]]
    hub_table = lax.all_gather(hub_mine, "dom", axis=0, tiled=True)
    table = jnp.concatenate([features, boundary, hub_table], axis=0)
    valid = jnp.concatenate(
        [jnp.ones((own_rows,), jnp.float32), in_valid, jnp.ones((hub_total,), jnp.float32)]
    )
    table_blocks = table.reshape(sources, tile_rows, width)
    valid_blocks = valid.reshape(sources, tile_rows)
    active = (jnp.arange(slots, dtype=jnp.int32)[None, :] < tile_count[:, None]).astype(jnp.float32)
    column_mask = valid_blocks[tile_src] * active[:, :, None]
    masked = tiles * column_mask[:, :, None, :].astype(jnp.bfloat16)
    picked = table_blocks[tile_src]
    numer = jnp.einsum("tkij,tkjf->tif", masked, picked, preferred_element_type=jnp.float32)
    degree = jnp.sum(masked, axis=(1, 3), dtype=jnp.float32).reshape(own_rows)
    agg = (numer.reshape(own_rows, width) / degree[:, None]).astype(jnp.bfloat16)
    pre = jnp.dot(features, w_self, preferred_element_type=jnp.float32) + jnp.dot(
        agg, w_neigh, preferred_element_type=jnp.float32
    )
    sigmoid_pre = jax.nn.sigmoid(pre)
    layer_out = (pre * sigmoid_pre).astype(jnp.bfloat16)
    grad_pre = (
        cotangent.astype(jnp.float32) * sigmoid_pre * (1.0 + pre * (1.0 - sigmoid_pre))
    ).astype(jnp.bfloat16)
    self_local = jnp.dot(features.T, grad_pre, preferred_element_type=jnp.float32)
    neigh_local = jnp.dot(agg.T, grad_pre, preferred_element_type=jnp.float32)
    self_total, neigh_total = lax.psum((self_local, neigh_local), "dom")
    share = width // groups
    grad_w_self = lax.dynamic_slice_in_dim(self_total, position * share, share, 0)
    grad_w_neigh = lax.dynamic_slice_in_dim(neigh_total, position * share, share, 0)
    grad_scaled = (
        jnp.dot(grad_pre, w_neigh.T, preferred_element_type=jnp.float32) / degree[:, None]
    ).astype(jnp.bfloat16)
    grad_scaled = grad_scaled.reshape(blocks_own, tile_rows, width)
    back_terms = jnp.einsum(
        "tkij,tif->tkjf", masked, grad_scaled, preferred_element_type=jnp.float32
    )
    placement = (
        tile_src[:, :, None] == jnp.arange(sources, dtype=jnp.int32)[None, None, :]
    ).astype(jnp.float32)
    grad_source = jnp.einsum(
        "tks,tkjf->sjf", placement, back_terms, precision=lax.Precision.HIGHEST
    )
    grad_source = grad_source.reshape(sources * tile_rows, width)
    grad_features = (
        jnp.dot(grad_pre, w_self.T, preferred_element_type=jnp.float32) + grad_source[:own_rows]
    )
    bnd_grads = grad_source[own_rows : own_rows + bnd_rows].reshape(groups, cap_rows, width)
    returned = lax.all_to_all(
        bnd_grads.astype(jnp.bfloat16), "dom", split_axis=0, concat_axis=0, tiled=True
    ).astype(bnd_grads.dtype)
    returned = returned * out_valid[:, :, None].astype(jnp.float32)
    grad_features = grad_features.at[rows_out.reshape(-1)].add(returned.reshape(bnd_rows, width))
    hub_back = lax.psum_scatter(
        grad_source[own_rows + bnd_rows :], "dom", scatter_dimension=0, tiled=True
    )
    grad_features = grad_features.at[hub_rows[0]].add(hub_back)
    return (layer_out, grad_features, grad_w_self, grad_w_neigh)


def solution(mesh):
    in_specs = (
        P("dom", None),
        P(),
        P(),
        P("dom", None),
        P("dom", None, None, None),
        P("dom", None),
        P("dom"),
        P("dom", None, None),
        P("dom", None),
        P("dom", None),
    )
    out_specs = (P("dom", None), P("dom", None), P("dom", None), P("dom", None))
    return jax.shard_map(
        on_device, mesh=mesh, in_specs=in_specs, out_specs=out_specs, check_vma=False
    )
```

profile of v0, /device:TPU:0, one launch (start us, length us, event | category | flops | bytes accessed | tf_op | source)
XLA Modules:
  0.0 356.1 jit_solution(10724466520859372223)
XLA Ops:
  7.2 1.5 copy.34
  8.6 7.3 %all-to-all-start = ((s32[32,1,1]{2,1,0:T(1,128)}), s32[32,1,1]{2,1,0:T(1,128)S(1)}, u32[]{:S(2)}, u32[]{:S(2)}) async-start(s32[32,1,1]{2,1,0:T(1,128)} %copy.34), calls=%async_computation | async-start | bytes 32768 | tf_op jit(solution)/shard_map/all_to_all | solution.py:35
  15.9 0.7 fusion.20
  16.6 0.7 compare_select_fusion
  17.4 0.1 reshape.220
  17.5 1.3 fusion.21
  18.8 0.7 compare_select_fusion.2
  19.6 4.8 %gather_fusion.1 = bf16[512,768]{1,0:T(8,128)(2,1)} fusion(bf16[1024,768]{1,0:T(8,128)(2,1)} %param.10, s32[1024]{0:T(1024)S(1)} %pad_clamp_fusion.1), kind=kCustom, calls=%fused_computation.1 | custom fusion | bytes 1574912 | tf_op jit(solution)/shard_map/gather | solution.py:32
  24.4 2.2 broadcast_select_fusion
  26.7 0.6 gather_fusion.2
  27.3 6.0 %all-to-all-start.1 = ((bf16[32,16,768]{2,1,0:T(8,128)(2,1)}), bf16[32,16,768]{2,1,0:T(8,128)(2,1)}, u32[]{:S(2)}, u32[]{:S(2)}) async-start(bf16[32,16,768]{2,1,0:T(8,128)(2,1)} %broadcast_select_fusion), calls=%async_computation.1 | async-start | bytes 1572864 | tf_op jit(solution)/shard_map/all_to_all | solution.py:34
  33.3 48.5 %all-gather.1 = bf16[32,4,768]{2,1,0:T(4,128)(2,1)S(1)} all-gather(bf16[1,4,768]{2,1,0:T(4,128)(2,1)S(1)} %bitcast.70), channel_id=2, replica_groups=mesh['dom'=32] {'dom'}, dimensions={0}, use_global_device_ids=true | all-gather | bytes 202752 | tf_op jit(solution)/shard_map/all_gather | solution.py:40
  81.9 5.1 %fusion.22 = f32[1024,1024]{1,0:T(8,128)} fusion(bf16[1024,768]{1,0:T(8,128)(2,1)S(1)} %copy-done.2, bf16[768,1024]{1,0:T(8,128)(2,1)} %param.11), kind=kOutput, calls=%fused_computation.54 | convolution fusion | flops 1610612736 | bytes 7340032 | tf_op jit(solution)/shard_map/dot_general | solution.py:54
  87.0 0.7 reduce
  87.8 0.1 reshape.209
  87.9 0.6 gather_fusion
  88.5 2.1 convert_reduce_fusion
  90.6 2.8 pad_maximum_fusion
  93.4 9.2 %gather_fusion.3 = bf16[64,128,768]{2,1,0:T(8,128)(2,1)} fusion(bf16[13,128,768]{2,1,0:T(8,128)(2,1)} %bitcast.64, s32[1024]{0:T(1024)S(1)} %pad_clamp_fusion.2), kind=kCustom, calls=%fused_computation.3 | custom fusion | bytes 25166080 | tf_op jit(solution)/shard_map/gather | solution.py:50
  102.6 6.7 %fusion.8 = f32[8,128,768,1]{2,1,3,0:T(8,128)S(1)} fusion(bf16[8,8,128,768]{3,2,1,0:T(8,128)(2,1)} %bitcast.65, bf16[8,8,128,128]{3,2,1,0:T(8,128)(2,1)} %param.14, bf16[8,8,128]{2,1,0:T(8,128)(2,1)S(1)} %fusion.12), kind=kOutput, calls=%fused_computation.22 | convolution fusion | flops 1611661312 | bytes 17842176 | tf_op jit(solution)/shard_map/tkij,tkjf->tif/dot_general | solution.py:51
  109.3 0.3 fusion.2
  109.5 1.3 copy-done.14
  110.8 4.6 %multiply_convert_fusion = (bf16[1024,1024]{1,0:T(8,128)(2,1)S(1)}, bf16[1024,1024]{1,0:T(8,128)(2,1)}) fusion(bf16[1024,1024]{1,0:T(8,128)(2,1)S(1)} %copy-done.14, f32[1024,1024]{1,0:T(8,128)S(1)} %copy-done.16, bf16[1024,768]{1,0:T(8,128)(2,1)S(1)} %fusion.2, bf16[768,1024]{1,0:T(8,128)(2,1)S(1)} %copy-done), kind=kOutput, calls=%fused_computation.8 | convolution fusion | flops 1624244224 | bytes 13631488 | tf_op jit(solution)/shard_map/dot_general | solution.py:54
  115.5 1.8 divide_convert_fusion
  117.3 3.6 %convolution_bitcast_fusion = f32[768,1024]{0,1:T(8,128)} fusion(bf16[1024,1024]{1,0:T(8,128)(2,1)S(1)} %get-tuple-element.23, bf16[1024,768]{1,0:T(8,128)(2,1)S(1)} %copy-done.2), kind=kOutput, calls=%fused_computation.19 | convolution fusion | flops 1610612736 | bytes 6815744 | tf_op jit(solution)/shard_map/dot_general | solution.py:62
  120.9 3.6 %fusion.23 = f32[768,1024]{1,0:T(8,128)} fusion(bf16[1024,768]{1,0:T(8,128)(2,1)S(1)} %fusion.2, bf16[1024,1024]{1,0:T(8,128)(2,1)S(1)} %get-tuple-element.23), kind=kOutput, calls=%fused_computation.55 | convolution fusion | flops 1610612736 | bytes 6815744 | tf_op jit(solution)/shard_map/dot_general | solution.py:63
  124.5 10.1 %fusion.6 = f32[8,8,128,768]{3,2,1,0:T(8,128)} fusion(bf16[8,128,768,1]{2,1,3,0:T(8,128)(2,1)S(1)} %bitcast.68, bf16[8,8,128,128]{3,2,1,0:T(8,128)(2,1)S(1)} %copy-done.3, bf16[8,8,128]{2,1,0:T(8,128)(2,1)S(1)} %fusion.12), kind=kOutput, calls=%fused_computation.20 | convolution fusion | flops 1611661312 | bytes 28852224 | tf_op jit(solution)/shard_map/tkij,tif->tkjf/dot_general | solution.py:72
  134.6 28.1 %fusion.3 = f32[13,128,768]{2,0,1:T(8,128)S(1)} fusion(f32[8,8,128,768]{3,2,1,0:T(8,128)} %fusion.6, s32[8,8]{0,1:T(8,128)S(1)} %copy.36), kind=kOutput, calls=%fused_computation.16 | convolution fusion | flops 981467968 | bytes 30277888 | tf_op jit(solution)/shard_map/tks,tkjf->sjf/dot_general | solution.py:78
  162.7 2.7 copy-done.4
  165.3 0.4 slice.32
  165.7 0.8 copy.53
  166.5 2.1 slice.34
  168.7 1.0 copy.41
  169.7 2.9 all-to-all-start.2
  172.7 0.1 reshape_squeeze.3
  172.8 1.9 slice-done
  174.6 1.0 copy.39
  175.7 0.6 copy-done.6
  176.3 0.5 copy-done.15
  176.8 3.5 bitcast_add_fusion
  180.3 21.6 %all-to-all-done.2 = bf16[32,16,768]{2,1,0:T(8,128)(2,1)S(1)} async-done(((bf16[32,16,768]{2,1,0:T(8,128)(2,1)}), bf16[32,16,768]{2,1,0:T(8,128)(2,1)S(1)}, u32[]{:S(2)}, u32[]{:S(2)}) %all-to-all-start.2) | async-done | bytes 786464 | tf_op jit(solution)/shard_map/all_to_all | solution.py:86
  201.9 0.2 convert_multiply_fusion
  202.1 7.4 %scatter_fusion = f32[1024,768]{1,0:T(8,128)} fusion(f32[1024,768]{1,0:T(8,128)} %bitcast_add_fusion, s32[512]{0:T(512)S(1)} %bitcast.73, f32[512,768]{1,0:T(8,128)S(1)} %bitcast.66), kind=kCustom, calls=%fused_computation.4 | custom fusion | flops 393216 | bytes 4720640 | tf_op jit(solution)/shard_map/scatter-add | solution.py:90
  209.5 131.6 %all-reduce.4.cloned.1.call-done = (f32[128,768]{1,0:T(8,128)}, f32[768,1024]{0,1:T(8,128)}, f32[768,1024]{1,0:T(8,128)}) async-done(((f32[128,768]{1,0:T(8,128)}, f32[768,1024]{0,1:T(8,128)}, f32[768,1024]{1,0:T(8,128)}), (f32[128,768]{1,0:T(8,128)}, f32[768,1024]{0,1:T(8,128)}, f32[768,1024]{1,0:T(8,128)})) %all-reduce.4.cloned.1.call-update) | async-done | bytes 6684688
  341.0 1.5 constant_dynamic-slice_fusion.1
  342.6 0.8 copy.42
  343.4 1.5 constant_dynamic-slice_fusion
  344.9 4.3 %scatter_custom_fusion.1 = f32[1024,768]{1,0:T(8,128)} fusion(f32[1024,768]{1,0:T(8,128)} %scatter_fusion, s32[4]{0:T(128)} %copy-done.13, f32[128,768]{1,0:T(8,128)} %get-tuple-element.20, u32[]{:T(128)S(6)} %multiply.1, u32[]{:T(128)} %constant.7), kind=kCustom, calls=%fused_computation.39 | custom fusion | flops 3072 | bytes 3158532 | tf_op jit(solution)/shard_map/scatter-add | solution.py:94
  (50 shorter events, 0.7 us)
Async XLA Ops:
  7.2 102.4 %copy-start = (bf16[768,1024]{1,0:T(8,128)(2,1)S(1)}, bf16[768,1024]{1,0:T(8,128)(2,1)}, u32[]{:S(2)}) copy-start(bf16[768,1024]{1,0:T(8,128)(2,1)} %param.12) | copy-start | bytes 4718596
  8.6 18.6 %all-to-all-start = ((s32[32,1,1]{2,1,0:T(1,128)}), s32[32,1,1]{2,1,0:T(1,128)S(1)}, u32[]{:S(2)}, u32[]{:S(2)}) async-start(s32[32,1,1]{2,1,0:T(1,128)} %copy.34), calls=%async_computation | async-start | bytes 32768 | tf_op jit(solution)/shard_map/all_to_all | solution.py:35
  16.6 0.9 copy-start.13
  19.6 7.0 %copy-start.11 = (s32[8,8]{1,0:T(8,128)S(1)}, s32[8,8]{1,0:T(8,128)}, u32[]{:S(2)}) copy-start(s32[8,8]{1,0:T(8,128)} %param.15) | copy-start | bytes 772
  19.6 7.1 %copy-start.2 = (bf16[1024,768]{1,0:T(8,128)(2,1)S(1)}, bf16[1024,768]{1,0:T(8,128)(2,1)}, u32[]{:S(2)}) copy-start(bf16[1024,768]{1,0:T(8,128)(2,1)} %param.10) | copy-start | bytes 4718596
  24.4 57.4 %copy-start.12 = (s32[8]{0:T(128)S(1)}, s32[8]{0:T(128)}, u32[]{:S(2)}) copy-start(s32[8]{0:T(128)} %param.16) | copy-start | bytes 100
  27.2 6.0 %copy-start.8 = (s32[32,1,1]{2,1,0:T(1,128)}, s32[32,1,1]{2,1,0:T(1,128)S(1)}, u32[]{:S(2)}) copy-start(s32[32,1,1]{2,1,0:T(1,128)S(1)} %all-to-all-done) | copy-start | bytes 388
  27.3 63.4 %all-to-all-start.1 = ((bf16[32,16,768]{2,1,0:T(8,128)(2,1)}), bf16[32,16,768]{2,1,0:T(8,128)(2,1)}, u32[]{:S(2)}, u32[]{:S(2)}) async-start(bf16[32,16,768]{2,1,0:T(8,128)(2,1)} %broadcast_select_fusion), calls=%async_computation.1 | async-start | bytes 1572864 | tf_op jit(solution)/shard_map/all_to_all | solution.py:34
  33.2 307.8 %all-reduce.4.cloned.1.call-start = ((), (), s32[]{:S(2)}) async-start(), calls=%async_computation.3 | async-start | bytes 13369344
  81.9 5.1 %copy-start.9 = (s32[32,1,1]{2,1,0:T(1,128)S(1)}, s32[32,1,1]{2,1,0:T(1,128)}, u32[]{:S(2)}) copy-start(s32[32,1,1]{2,1,0:T(1,128)} %copy-done.8) | copy-start | bytes 388
  102.6 7.0 %copy-start.16 = (f32[1024,1024]{1,0:T(8,128)S(1)}, f32[1024,1024]{1,0:T(8,128)}, u32[]{:S(2)}) copy-start(f32[1024,1024]{1,0:T(8,128)} %fusion.22) | copy-start | bytes 12582916
  109.2 1.6 copy-start.14
  115.5 5.5 %copy-start.5 = (bf16[1024,1024]{1,0:T(8,128)(2,1)}, bf16[1024,1024]{1,0:T(8,128)(2,1)S(1)}, u32[]{:S(2)}) copy-start(bf16[1024,1024]{1,0:T(8,128)(2,1)S(1)} %get-tuple-element.23) | copy-start | bytes 6291460
  120.9 3.6 %copy-start.3 = (bf16[8,8,128,128]{3,2,1,0:T(8,128)(2,1)S(1)}, bf16[8,8,128,128]{3,2,1,0:T(8,128)(2,1)}, u32[]{:S(2)}) copy-start(bf16[8,8,128,128]{3,2,1,0:T(8,128)(2,1)} %param.14) | copy-start | bytes 6291460
  162.7 2.7 copy-start.4
  166.5 6.0 %copy-start.10 = (s32[1,32,16]{1,2,0:T(8,128)S(1)}, s32[1,32,16]{1,2,0:T(8,128)}, u32[]{:S(2)}) copy-start(s32[1,32,16]{1,2,0:T(8,128)} %param.17) | copy-start | bytes 6148
  169.7 32.2 %all-to-all-start.2 = ((bf16[32,16,768]{2,1,0:T(8,128)(2,1)}), bf16[32,16,768]{2,1,0:T(8,128)(2,1)S(1)}, u32[]{:S(2)}, u32[]{:S(2)}) async-start(bf16[32,16,768]{2,1,0:T(8,128)(2,1)} %bitcast.24), calls=%async_computation.2 | async-start | bytes 1572864 | tf_op jit(solution)/shard_map/all_to_all | solution.py:86
  172.7 1.9 slice-start
  174.6 1.6 copy-start.6
  174.6 2.1 copy-start.15
  176.8 25.1 %copy-start.7 = (f32[32,16]{1,0:T(8,128)S(1)}, f32[32,16]{1,0:T(8,128)}, u32[]{:S(2)}) copy-start(f32[32,16]{1,0:T(8,128)} %get-tuple-element.25) | copy-start | bytes 6148
  341.0 8.2 %copy-start.1 = (bf16[768,1024]{1,0:T(8,128)(2,1)S(1)}, bf16[768,1024]{1,0:T(8,128)(2,1)}, u32[]{:S(2)}) copy-start(bf16[768,1024]{1,0:T(8,128)(2,1)} %param.12) | copy-start | bytes 4718596
Sparse Core Ops, SparseCore 0:
  166.7 174.3 all-reduce.3
where the time goes:
time: 357 us; the launch traced here: 356 us
  waiting for transfers between devices  153 us (43%)
  matrix products  67.1 us (19%)
  blocking collectives  48.5 us (14%)
  local copies, waits for them, and re-layouts  33.4 us (9%)
  other arithmetic  23.5 us (7%)
  starting transfers between devices  16.2 us (5%)
  between operations  14.3 us (4%)
    unnamed x2, waiting for transfers between devices  132 us
    all_gather x1, blocking collectives, on_device(): hub_table = lax.all_gather(hub_mine, 'dom', axis=0, tiled=True)  48.5 us
    dot_general x1, matrix products, on_device(): jnp.einsum('tks,tkjf->sjf', placement, back_terms, precision=lax.Precisio...  28.1 us
    all_to_all x1, waiting for transfers between devices, on_device(): lax.all_to_all(bnd_grads.astype(jnp.bfloat16), 'dom', split_axis=0, conca...  21.6 us
    dot_general x1, matrix products, on_device(): jnp.einsum('tkij,tif->tkjf', masked, grad_scaled, preferred_element_type=...  10.1 us
    gather x1, local copies, waits for them, and re-layouts, on_device(): picked = table_blocks[tile_src]  9.18 us
    scatter-add x1, other arithmetic, on_device(): grad_features.at[rows_out.reshape(-1)]  7.38 us
    all_to_all x1, starting transfers between devices, on_device(): lax.all_to_all(counts_out[:, None], 'dom', split_axis=0, concat_axis=0, t...  7.3 us
  transfers between devices with their start and end apart: 4, of which 2 were waited for; matrix products, arithmetic and copies ran while one was open for 10% of the time, Pallas kernels for 0%

commit v1 on v0

--- a/solution.py
+++ b/solution.py
@@ -1,7 +1,358 @@
+import functools
+
 import jax
 import jax.numpy as jnp
 from jax import lax
+from jax.experimental import pallas as pl
+from jax.experimental.pallas import tpu as pltpu
 from jax.sharding import PartitionSpec as P
+
+BF16 = jnp.bfloat16
+F32 = jnp.float32
+LANES = 128
+MIB = 1 << 20
+
+
+def mm(a, b, contract=((1,), (0,))):
+    return lax.dot_general(a, b, (contract, ((), ())), preferred_element_type=F32)
+
+
+def params(mib):
+    return pltpu.CompilerParams(vmem_limit_bytes=mib * MIB)
+
+
+def cost(flops, moved):
+    return pl.CostEstimate(flops=flops, bytes_accessed=moved, transcendentals=0)
+
+
+def pack_kernel(caps, idx_ref, feat_ref, out_ref):
+    parts, _, _ = out_ref.shape
+    bnd = parts * caps
+    idx = idx_ref[...]
+    rows = feat_ref.shape[0]
+    hit = lax.broadcasted_iota(jnp.int32, (idx.shape[0], rows), 1) == idx
+    picked = mm(jnp.where(hit, 1.0, 0.0).astype(BF16), feat_ref[...])
+    picked = jnp.where(idx >= 0, picked, jnp.inf)
+    groups = picked.shape[1] // LANES
+    sub = lax.broadcasted_iota(jnp.int32, (8, LANES), 0)
+    hubs = []
+    for g in range(groups):
+        piece = picked[:bnd, g * LANES : (g + 1) * LANES].astype(BF16)
+        out_ref[:, g * caps : (g + 1) * caps, :] = piece.reshape(parts, caps, LANES)
+        hubs.append(picked[bnd : bnd + 8, g * LANES : (g + 1) * LANES])
+    rows_hub = [jnp.where(sub < 4, hubs[2 * j], hubs[2 * j + 1]) for j in range(groups // 2)]
+    block = jnp.concatenate(rows_hub, axis=0).astype(BF16)
+    out_ref[:, groups * caps :, :] = jnp.broadcast_to(block[None], (parts, groups * 4, LANES))
+
+
+def early_kernel(src_ref, count_ref, tiles_ref, feat_ref, rows_ref, w_ref, *rest):
+    own_ref, bnd_ref, own_t_ref, bnd_t_ref, numer_ref, degree_ref, pre_ref, acc = rest
+    step = pl.program_id(0)
+    here, slots, tile, _ = tiles_ref.shape
+    own = own_ref.shape[1]
+    acc[...] = jnp.zeros_like(acc)
+    for t in range(here):
+        block = step * here + t
+        for k in range(slots):
+
+            @pl.when(k < count_ref[block])
+            def _():
+                at = pl.ds(pl.multiple_of(src_ref[block, k] * tile, tile), tile)
+                acc[t * tile : (t + 1) * tile, at] += tiles_ref[t, k].astype(F32)
+
+    dense = acc[...].astype(BF16)
+    own_ref[...] = dense[:, :own]
+    bnd_ref[...] = dense[:, own:]
+    flipped = dense.T
+    own_t_ref[...] = flipped[:own]
+    bnd_t_ref[...] = flipped[own:]
+    numer_ref[...] = mm(dense[:, :own], feat_ref[...])
+    degree_ref[...] = mm(dense[:, :own], jnp.ones((own, LANES), BF16))
+    pre_ref[...] = mm(rows_ref[...], w_ref[...])
+
+
+def unpack_table(caps, got_ref, table):
+    parts = got_ref.shape[0]
+    bnd = parts * caps
+    width = table.shape[1] - LANES
+    groups = width // LANES
+    for g in range(groups):
+        piece = got_ref[:, g * caps : (g + 1) * caps, :].astype(F32).reshape(bnd, LANES)
+        used = piece < jnp.inf
+        table[:bnd, g * LANES : (g + 1) * LANES] = jnp.where(used, piece, 0.0).astype(BF16)
+        if g == 0:
+            table[:bnd, width:] = jnp.where(used, 1.0, 0.0).astype(BF16)
+    hub_rows = groups * 4
+    hubs = got_ref[:, groups * caps :, :].astype(F32).reshape(parts * hub_rows, LANES)
+    down = pltpu.roll(hubs, 4, 0).reshape(parts // 2, 2 * hub_rows, LANES)
+    up = pltpu.roll(hubs, parts * hub_rows - 4, 0).reshape(parts // 2, 2 * hub_rows, LANES)
+    hubs = hubs.reshape(parts // 2, 2 * hub_rows, LANES)
+    low = lax.broadcasted_iota(jnp.int32, (parts // 2, hub_rows, LANES), 1) % 8 < 4
+    even = jnp.where(low, hubs[:, :hub_rows], down[:, hub_rows:]).astype(BF16)
+    odd = jnp.where(low, up[:, :hub_rows], hubs[:, hub_rows:]).astype(BF16)
+    for g in range(groups):
+        half = even if g % 2 == 0 else odd
+        j = g // 2
+        piece = half[:, 8 * j : 8 * j + 8, :].reshape(parts * 4, LANES)
+        table[bnd:, g * LANES : (g + 1) * LANES] = piece
+    table[bnd:, width:] = jnp.ones((parts * 4, LANES), BF16)
+
+
+def main_kernel(caps, got_ref, bnd_ref, numer_ref, degree_ref, pre_ref, w_ref, cot_ref, *rest):
+    out_ref, gp_ref, agg_ref, inv_ref, table = rest
+
+    @pl.when(pl.program_id(0) == 0)
+    def _():
+        unpack_table(caps, got_ref, table)
+
+    width = numer_ref.shape[1]
+    adj = bnd_ref[...]
+    numer = numer_ref[...] + mm(adj, table[:, :width])
+    inv = 1.0 / (degree_ref[...] + mm(adj, table[:, width:]))
+    inv_ref[...] = inv
+    agg = (numer * jnp.concatenate([inv] * (width // LANES), axis=1)).astype(BF16)
+    agg_ref[...] = agg
+    pre = pre_ref[...] + mm(agg, w_ref[...])
+    sig = jax.nn.sigmoid(pre)
+    out_ref[...] = (pre * sig).astype(BF16)
+    gp_ref[...] = (cot_ref[...].astype(F32) * sig * (1.0 + pre * (1.0 - sig))).astype(BF16)
+
+
+def weight_kernel(masks, x_ref, gp_ref, keep_ref, send_ref, acc):
+    me = lax.axis_index("dom")
+    acc[...] = mm(x_ref[...], gp_ref[...], ((0,), (0,)))
+    share = keep_ref.shape[1]
+    for p, mask in enumerate(masks):
+        mine = jnp.bitwise_xor(me, mask)
+        other = jnp.bitwise_xor(me, mask + 1)
+        keep_ref[p] = acc[pl.ds(pl.multiple_of(mine * share, 8), share), :]
+        send_ref[p] = acc[pl.ds(pl.multiple_of(other * share, 8), share), :].astype(BF16)
+
+
+def back_kernel(caps, gp_ref, w_ref, inv_ref, bnd_t_ref, gs_ref, out_ref):
+    parts = out_ref.shape[0]
+    bnd = parts * caps
+    width = gs_ref.shape[1]
+    groups = width // LANES
+    inv = inv_ref[...]
+    scaled = mm(gp_ref[...], w_ref[...], ((1,), (1,)))
+    gs = (scaled * jnp.concatenate([inv] * groups, axis=1)).astype(BF16)
+    gs_ref[...] = gs
+    grads = mm(bnd_t_ref[...], gs)
+    for g in range(groups):
+        piece = grads[:bnd, g * LANES : (g + 1) * LANES].astype(BF16)
+        out_ref[:, g * caps : (g + 1) * caps, :] = piece.reshape(parts, caps, LANES)
+    half = parts // 2
+    low = lax.broadcasted_iota(jnp.int32, (half, 8, LANES), 1) < 4
+    even, odd = [], []
+    for j in range(groups // 2):
+        a = grads[bnd:, 2 * j * LANES : (2 * j + 1) * LANES]
+        b = grads[bnd:, (2 * j + 1) * LANES : (2 * j + 2) * LANES]
+        up = pltpu.roll(a, parts * 4 - 4, 0).reshape(half, 8, LANES)
+        down = pltpu.roll(b, 4, 0).reshape(half, 8, LANES)
+        a, b = a.reshape(half, 8, LANES), b.reshape(half, 8, LANES)
+        even.append(jnp.where(low, a, down))
+        odd.append(jnp.where(low, up, b))
+    even = jnp.concatenate(even, axis=1)
+    odd = jnp.concatenate(odd, axis=1)
+    hubs = jnp.concatenate([even, odd], axis=1).reshape(parts, groups * 4, LANES)
+    out_ref[:, groups * caps :, :] = hubs.astype(BF16)
+
+
+def own_kernel(gp_ref, w_ref, own_t_ref, gs_ref, out_ref):
+    out_ref[...] = mm(gp_ref[...], w_ref[...], ((1,), (1,))) + mm(own_t_ref[...], gs_ref[...])
+
+
+def final_kernel(caps, hub_ref, own_ref, got_ref, idx_ref, out_ref, rows):
+    parts = got_ref.shape[0]
+    bnd = parts * caps
+    width = out_ref.shape[1]
+    groups = width // LANES
+    for g in range(groups):
+        piece = got_ref[:, g * caps : (g + 1) * caps, :]
+        rows[:, g * LANES : (g + 1) * LANES] = piece.reshape(bnd, LANES)
+    hit = lax.broadcasted_iota(jnp.int32, (out_ref.shape[0], bnd), 0) == idx_ref[...]
+    out_ref[...] = own_ref[...] + mm(jnp.where(hit, 1.0, 0.0).astype(BF16), rows[...])
+    hubs = jnp.sum(got_ref[:, groups * caps :, :].astype(F32), axis=0)
+    for i in range(4):
+        row = jnp.concatenate([hubs[4 * g + i : 4 * g + i + 1] for g in range(groups)], axis=1)
+        out_ref[pl.ds(hub_ref[0, i], 1), :] += row
+
+
+def swap(x, mask, parts):
+    return lax.ppermute(x, "dom", [(d, d ^ mask) for d in range(parts)])
+
+
+VMEM = pl.BlockSpec(memory_space=pltpu.VMEM)
+SMEM = pl.BlockSpec(memory_space=pltpu.SMEM)
+
+
+def on_device_fast(
+    features,
+    w_self,
+    w_neigh,
+    cotangent,
+    tiles,
+    tile_src,
+    tile_count,
+    send_rows,
+    send_count,
+    hub_rows,
+):
+    parts = lax.axis_size("dom")
+    rows, width = features.shape
+    hidden = w_self.shape[1]
+    blocks, slots, tile, _ = tiles.shape
+    caps = send_rows.shape[2]
+    hub_own = hub_rows.shape[1]
+    bnd = parts * caps
+    far = bnd + parts * hub_own
+    groups = width // LANES
+    sent_rows = groups * (caps + hub_own)
+    shape = jax.ShapeDtypeStruct
+
+    used = jnp.arange(caps, dtype=jnp.int32)[None, :] < send_count[0][:, None]
+    idx = jnp.where(used, send_rows[0], -1)
+    idx_col = jnp.concatenate([idx.reshape(bnd), hub_rows[0], hub_rows[0], hub_rows[0], hub_rows[0]])
+    idx_col = idx_col.reshape(bnd + 16, 1)
+    idx_row = idx.reshape(1, bnd)
+
+    outgoing = pl.pallas_call(
+        functools.partial(pack_kernel, caps),
+        out_shape=shape((parts, sent_rows, LANES), BF16),
+        in_specs=[VMEM, VMEM],
+        out_specs=VMEM,
+        compiler_params=params(24),
+        cost_estimate=cost(2 * bnd * rows * width, 4 * MIB),
+        name="pack",
+    )(idx_col, features)
+    got = lax.all_to_all(outgoing, "dom", split_axis=0, concat_axis=0, tiled=True)
+
+    steps = 4
+    per = rows // steps
+    row_block = lambda n: pl.BlockSpec((per, n), lambda s: (s, 0))
+    col_block = lambda n: pl.BlockSpec((n, per), lambda s: (0, s))
+    whole = lambda *n: pl.BlockSpec(n, lambda s: (0,) * len(n))
+    own_adj, bnd_adj, own_adj_t, bnd_adj_t, numer, degree, pre_self = pl.pallas_call(
+        early_kernel,
+        grid=(steps,),
+        out_shape=(
+            shape((rows, rows), BF16),
+            shape((rows, far), BF16),
+            shape((rows, rows), BF16),
+            shape((far, rows), BF16),
+            shape((rows, width), F32),
+            shape((rows, LANES), F32),
+            shape((rows, hidden), F32),
+        ),
+        in_specs=[
+            SMEM,
+            SMEM,
+            pl.BlockSpec((blocks // steps, slots, tile, tile), lambda s: (s, 0, 0, 0)),
+            whole(rows, width),
+            row_block(width),
+            whole(width, hidden),
+        ],
+        out_specs=(
+            row_block(rows),
+            row_block(far),
+            col_block(rows),
+            col_block(far),
+            row_block(width),
+            row_block(LANES),
+            row_block(hidden),
+        ),
+        scratch_shapes=[pltpu.VMEM((per, rows + far), F32)],
+        compiler_params=params(32),
+        cost_estimate=cost(6 * 10**9, 16 * MIB),
+        name="early",
+    )(tile_src, tile_count, tiles, features, features, w_self)
+
+    layer_out, grad_pre, agg, inv = pl.pallas_call(
+        functools.partial(main_kernel, caps),
+        grid=(steps,),
+        out_shape=(
+            shape((rows, hidden), BF16),
+            shape((rows, hidden), BF16),
+            shape((rows, width), BF16),
+            shape((rows, LANES), F32),
+        ),
+        in_specs=[
+            whole(parts, sent_rows, LANES),
+            row_block(far),
+            row_block(width),
+            row_block(LANES),
+            row_block(hidden),
+            whole(width, hidden),
+            row_block(hidden),
+        ],
+        out_specs=(row_block(hidden), row_block(hidden), row_block(width), row_block(LANES)),
+        scratch_shapes=[pltpu.VMEM((far, width + LANES), BF16)],
+        compiler_params=params(32),
+        cost_estimate=cost(4 * 10**9, 16 * MIB),
+        name="middle",
+    )(got, bnd_adj, numer, degree, pre_self, w_neigh, cotangent)
+
+    share = width // parts
+    half = parts // 2
+
+    def weight_partial(x, first, second, name):
+        masks = [first * (p >> 3) | second * (p >> 2 & 1) | (p & 3) << 3 for p in range(half)]
+        return pl.pallas_call(
+            functools.partial(weight_kernel, masks),
+            out_shape=(shape((half, share, hidden), F32), shape((half, share, hidden), BF16)),
+            in_specs=[VMEM, VMEM],
+            out_specs=(VMEM, VMEM),
+            scratch_shapes=[pltpu.VMEM((width, hidden), F32)],
+            compiler_params=params(32),
+            cost_estimate=cost(2 * rows * width * hidden, 10 * MIB),
+            name=name,
+        )(x, grad_pre)
+
+    def plane_sum(keep, send, first, second):
+        total = keep + swap(send, 1, parts).astype(F32)
+        total = total[:8] + swap(total[8:].astype(BF16), first, parts).astype(F32)
+        return total[:4] + swap(total[4:].astype(BF16), second, parts).astype(F32)
+
+    keep_s, send_s = weight_partial(features, 2, 4, "weight_self")
+    keep_n, send_n = weight_partial(agg, 4, 2, "weight_neigh")
+    plane = jnp.stack([plane_sum(keep_s, send_s, 2, 4), plane_sum(keep_n, send_n, 4, 2)])
+    total = plane[:, 0]
+    for far_z in range(1, 4):
+        total = total + swap(plane[:, far_z].astype(BF16), far_z << 3, parts).astype(F32)
+
+    gs, back = pl.pallas_call(
+        functools.partial(back_kernel, caps),
+        out_shape=(shape((rows, width), BF16), shape((parts, sent_rows, LANES), BF16)),
+        in_specs=[VMEM] * 4,
+        out_specs=(VMEM, VMEM),
+        compiler_params=params(32),
+        cost_estimate=cost(3 * 10**9, 8 * MIB),
+        name="back",
+    )(grad_pre, w_neigh, inv, bnd_adj_t)
+    returned = lax.all_to_all(back, "dom", split_axis=0, concat_axis=0, tiled=True)
+
+    own_grad = pl.pallas_call(
+        own_kernel,
+        out_shape=shape((rows, width), F32),
+        in_specs=[VMEM] * 4,
+        out_specs=VMEM,
+        compiler_params=params(32),
+        cost_estimate=cost(3 * 10**9, 10 * MIB),
+        name="own",
+    )(grad_pre, w_self, own_adj_t, gs)
+
+    grad_features = pl.pallas_call(
+        functools.partial(final_kernel, caps),
+        out_shape=shape((rows, width), F32),
+        in_specs=[SMEM, VMEM, VMEM, VMEM],
+        out_specs=VMEM,
+        scratch_shapes=[pltpu.VMEM((bnd, width), BF16)],
+        compiler_params=params(32),
+        cost_estimate=cost(10**9, 8 * MIB),
+        name="final",
+    )(hub_rows, own_grad, returned, idx_row)
+    return layer_out, grad_features, total[0], total[1]
 
 
 def on_device(
@@ -95,6 +446,15 @@
     return (layer_out, grad_features, grad_w_self, grad_w_neigh)
 
 
+def on_any_device(*args):
+    features, send_rows, hub_rows = args[0], args[7], args[9]
+    parts = lax.axis_size("dom")
+    share = features.shape[1] // parts
+    if parts == 32 and share % 8 == 0 and send_rows.shape[2] % 16 == 0 and hub_rows.shape[1] == 4:
+        return on_device_fast(*args)
+    return on_device(*args)
+
+
 def solution(mesh):
     in_specs = (
         P("dom", None),
@@ -110,5 +470,5 @@
     )
     out_specs = (P("dom", None), P("dom", None), P("dom", None), P("dom", None))
     return jax.shard_map(
-        on_device, mesh=mesh, in_specs=in_specs, out_specs=out_specs, check_vma=False
-    )
+        on_any_device, mesh=mesh, in_specs=in_specs, out_specs=out_specs, check_vma=False
+    )

time: 357 us -> 115 us (0.32)
  waiting for transfers between devices: 153 us -> 24.1 us
  matrix products: 67.1 us -> 0 us
  blocking collectives: 48.5 us -> 0 us
  Pallas kernels: 0 us -> 32.8 us
  other arithmetic: 23.5 us -> 6.52 us
  between operations: 14.3 us -> 0.95 us
  local copies, waits for them, and re-layouts: 33.4 us -> 28.2 us
  starting transfers between devices: 16.2 us -> 21.3 us
    unnamed x2 -> x0, waiting for transfers between devices: 132 us -> none
    dot_general x9 -> x0, matrix products: 67.1 us -> none  [the longest x1 28.1 us: on_device(): jnp.einsum('tks,tkjf->sjf', placement, back_terms, precision=lax.Precisio...]
    all_gather x1 -> x0, blocking collectives: 48.5 us -> none  [on_device(): hub_table = lax.all_gather(hub_mine, 'dom', axis=0, tiled=True)]
    pallas_call x0 -> x8, Pallas kernels: none -> 32.8 us  [the longest x1 7.29 us: on_device_fast(): pl.pallas_call(early_kernel, grid=(steps,), out_shape=(shape((rows, rows)...]
    unnamed x39 -> x69, local copies, waits for them, and re-layouts: 6.91 us -> 26 us
    ppermute x0 -> x9, waiting for transfers between devices: none -> 17.3 us  [swap(): return lax.ppermute(x, 'dom', [(d, d ^ mask) for d in range(parts)])]
    gather x4 -> x0, local copies, waits for them, and re-layouts: 15.2 us -> none  [the longest x1 9.18 us: on_device(): picked = table_blocks[tile_src]]
    all_to_all x3 -> x2, waiting for transfers between devices: 21.6 us -> 6.75 us  [the longest x1 6.75 us: on_device_fast(): lax.all_to_all(outgoing, 'dom', split_axis=0, concat_axis=0, tiled=True)]
  transfers between devices with their start and end apart: 4 -> 11, of which waited for: 2 -> 6; matrix products, arithmetic and copies ran while one was open for 10% -> 6% of each run, Pallas kernels for 0% -> 15%
where the time goes in v1:
time: 115 us; the launch traced here: 114 us
  Pallas kernels  32.8 us (29%)
  local copies, waits for them, and re-layouts  28.2 us (25%)
  waiting for transfers between devices  24.1 us (21%)
  starting transfers between devices  21.3 us (19%)
  other arithmetic  6.52 us (6%)
    unnamed x69, local copies, waits for them, and re-layouts  26 us
    ppermute x9, waiting for transfers between devices, swap(): return lax.ppermute(x, 'dom', [(d, d ^ mask) for d in range(parts)])  17.3 us
    ppermute x9, starting transfers between devices, swap(): return lax.ppermute(x, 'dom', [(d, d ^ mask) for d in range(parts)])  11.2 us
    all_to_all x1, starting transfers between devices, on_device_fast(): lax.all_to_all(outgoing, 'dom', split_axis=0, concat_axis=0, tiled=True)  7.29 us
    pallas_call x1, Pallas kernels, on_device_fast(): pl.pallas_call(early_kernel, grid=(steps,), out_shape=(shape((rows, rows)...  7.29 us
    pallas_call x1, Pallas kernels, on_device_fast(): pl.pallas_call(functools.partial(main_kernel, caps), grid=(steps,), out_s...  7.01 us
    all_to_all x1, waiting for transfers between devices, on_device_fast(): lax.all_to_all(outgoing, 'dom', split_axis=0, concat_axis=0, tiled=True)  6.75 us
    pallas_call x2, Pallas kernels, weight_partial(): pl.pallas_call(functools.partial(weight_kernel, masks), out_shape=(shape(...  5.78 us
  transfers between devices with their start and end apart: 11, of which 6 were waited for; matrix products, arithmetic and copies ran while one was open for 6% of the time, Pallas kernels for 15%

profile of v1, /device:TPU:0, one launch (start us, length us, event | category | flops | bytes accessed | tf_op | source)
XLA Modules:
  0.0 113.8 jit_solution(15556357679912226148)
XLA Ops:
  0.6 0.7 iota_compare_fusion
  1.5 0.8 copy.18
  2.3 0.9 concatenate.3
  3.3 1.4 %copy-done.5 = bf16[1024,768]{1,0:T(8,128)(2,1)S(1)} copy-done((bf16[1024,768]{1,0:T(8,128)(2,1)S(1)}, bf16[1024,768]{1,0:T(8,128)(2,1)}, u32[]{:S(2)}) %copy-start.5) | copy-done | bytes 1572888
  4.7 2.1 %pack.1 = bf16[32,120,128]{2,1,0:T(8,128)(2,1)} custom-call(s32[528,1]{1,0:T(8,128)S(1)} %reshape.54.idx_ref, bf16[1024,768]{1,0:T(8,128)(2,1)S(1)} %copy-done.5), custom_call_target="tpu_custom_call" | custom-call | flops 805306368 | bytes 4194304 | tf_op jit(solution)/shard_map/pack/pallas_call | solution.py:220
  6.9 7.3 %all-to-all-start = ((bf16[32,120,128]{2,1,0:T(8,128)(2,1)}), bf16[32,120,128]{2,1,0:T(8,128)(2,1)S(1)}, u32[]{:S(2)}, u32[]{:S(2)}) async-start(bf16[32,120,128]{2,1,0:T(8,128)(2,1)} %pack.1), calls=%async_computation | async-start | bytes 1966080 | tf_op jit(solution)/shard_map/all_to_all | solution.py:229
  14.2 1.4 %copy-done.6 = bf16[1024,768]{1,0:T(8,128)(2,1)S(1)} copy-done((bf16[1024,768]{1,0:T(8,128)(2,1)S(1)}, bf16[1024,768]{1,0:T(8,128)(2,1)}, u32[]{:S(2)}) %copy-start.6) | copy-done | bytes 1572888
  15.6 1.4 %copy-done.10 = bf16[768,1024]{1,0:T(8,128)(2,1)S(1)} copy-done((bf16[768,1024]{1,0:T(8,128)(2,1)S(1)}, bf16[768,1024]{1,0:T(8,128)(2,1)}, u32[]{:S(2)}) %copy-start.10) | copy-done | bytes 1572888
  17.0 7.3 %early.1 = (bf16[1024,1024]{1,0:T(8,128)(2,1)}, bf16[1024,640]{1,0:T(8,128)(2,1)S(1)}, bf16[1024,1024]{1,0:T(8,128)(2,1)S(1)}, bf16[640,1024]{1,0:T(8,128)(2,1)S...) custom-call(s32[8,8]{1,0:T(8,128)S(1)} %copy-done.12, s32[8]{0:T(128)S(1)} %copy-done.13, ...), custom_call_target="tpu_custom_call" | custom-call | flops 6000000000 | bytes 16777216 | tf_op jit(solution)/shard_map/early/pallas_call | solution.py:236
  24.4 1.3 %copy-done.14 = bf16[1024,1024]{1,0:T(8,128)(2,1)} copy-done((bf16[1024,1024]{1,0:T(8,128)(2,1)}, bf16[1024,1024]{1,0:T(8,128)(2,1)S(1)}, u32[]{:S(2)}) %copy-start.14) | copy-done | bytes 2097176
  25.7 2.0 %copy-done.19 = f32[1024,1024]{1,0:T(8,128)} copy-done((f32[1024,1024]{1,0:T(8,128)}, f32[1024,1024]{1,0:T(8,128)S(1)}, u32[]{:S(2)}) %copy-start.19) | copy-done | bytes 4194328
  27.7 1.7 %copy-done.21 = f32[1024,768]{1,0:T(8,128)} copy-done((f32[1024,768]{1,0:T(8,128)}, f32[1024,768]{1,0:T(8,128)S(1)}, u32[]{:S(2)}) %copy-start.21) | copy-done | bytes 3145752
  29.3 1.1 copy-done.23
  30.4 0.8 copy-done.27
  31.2 1.1 copy-done.29
  32.3 6.7 %all-to-all-done.got_ref = bf16[32,120,128]{2,1,0:T(8,128)(2,1)S(1)} async-done(((bf16[32,120,128]{2,1,0:T(8,128)(2,1)}), bf16[32,120,128]{2,1,0:T(8,128)(2,1)S(1)}, u32[]{:S(2)}, u32[]{:S(2)}) %all-to-all-start) | async-done | bytes 983072 | tf_op jit(solution)/shard_map/all_to_all | solution.py:229
  39.0 1.6 %copy-done.4 = bf16[1024,1024]{1,0:T(8,128)(2,1)S(1)} copy-done((bf16[1024,1024]{1,0:T(8,128)(2,1)S(1)}, bf16[1024,1024]{1,0:T(8,128)(2,1)}, u32[]{:S(2)}) %copy-start.4) | copy-done | bytes 2097176
  40.6 1.4 %copy-done.8 = bf16[768,1024]{1,0:T(8,128)(2,1)S(1)} copy-done((bf16[768,1024]{1,0:T(8,128)(2,1)S(1)}, bf16[768,1024]{1,0:T(8,128)(2,1)}, u32[]{:S(2)}) %copy-start.8) | copy-done | bytes 1572888
  42.0 2.2 %copy-done.20 = f32[1024,1024]{1,0:T(8,128)S(1)} copy-done((f32[1024,1024]{1,0:T(8,128)S(1)}, f32[1024,1024]{1,0:T(8,128)}, u32[]{:S(2)}) %copy-start.20) | copy-done | bytes 4194328
  44.2 1.9 %copy-done.22 = f32[1024,768]{1,0:T(8,128)S(1)} copy-done((f32[1024,768]{1,0:T(8,128)S(1)}, f32[1024,768]{1,0:T(8,128)}, u32[]{:S(2)}) %copy-start.22) | copy-done | bytes 3145752
  46.1 1.3 %copy-done.24 = bf16[1024,640]{1,0:T(8,128)(2,1)S(1)} copy-done((bf16[1024,640]{1,0:T(8,128)(2,1)S(1)}, bf16[1024,640]{1,0:T(8,128)(2,1)}, u32[]{:S(2)}) %copy-start.24) | copy-done | bytes 1310744
  47.4 1.0 copy-done.28
  48.5 7.0 %middle.1 = (bf16[1024,1024]{1,0:T(8,128)(2,1)}, bf16[1024,1024]{1,0:T(8,128)(2,1)S(1)}, bf16[1024,768]{1,0:T(8,128)(2,1)S(1)}, f32[1024,128]{1,0:T(8,128)S(1)}) custom-call(bf16[32,120,128]{2,1,0:T(8,128)(2,1)S(1)} %all-to-all-done.got_ref, bf16[1024,640]{1,0:T(8,128)(2,1)S(1)} %copy-done.24, f32[1024,768]{1,0:T(8,128)S(1)} %copy-done.22, ...), custom_call_target="tpu_custom_call" | custom-call | flops 4000000000 | bytes 16777216 | tf_op jit(solution)/shard_map/middle/pallas_call | solution.py:271
  55.5 2.9 %weight_self.1 = (f32[16,24,1024]{2,1,0:T(8,128)S(1)}, bf16[16,24,1024]{2,1,0:T(8,128)(2,1)}) custom-call(bf16[1024,768]{1,0:T(8,128)(2,1)S(1)} %copy-done.7, bf16[1024,1024]{1,0:T(8,128)(2,1)S(1)} %get-tuple-element.25.gp_ref), custom_call_target="tpu_custom_call" | custom-call | flops 1610612736 | bytes 10485760 | tf_op jit(solution)/shard_map/weight_self/pallas_call | solution.py:301
  58.4 2.9 %weight_neigh.1 = (f32[16,24,1024]{2,1,0:T(8,128)S(1)}, bf16[16,24,1024]{2,1,0:T(8,128)(2,1)}) custom-call(bf16[1024,768]{1,0:T(8,128)(2,1)S(1)} %get-tuple-element.33.x_ref, bf16[1024,1024]{1,0:T(8,128)(2,1)S(1)} %get-tuple-element.25.gp_ref), custom_call_target="tpu_custom_call" | custom-call | flops 1610612736 | bytes 10485760 | tf_op jit(solution)/shard_map/weight_neigh/pallas_call | solution.py:301
  61.3 0.5 collective-permute-start.3
  62.0 1.4 %convert_add_fusion.1 = f32[16,24,1024]{2,1,0:T(8,128)S(1)} fusion(f32[16,24,1024]{2,1,0:T(8,128)S(1)} %get-tuple-element.31, bf16[16,24,1024]{2,1,0:T(8,128)(2,1)} %collective-permute-done), kind=kLoop, calls=%fused_computation.1 | loop fusion | flops 786432 | bytes 3932160 | tf_op jit(solution)/shard_map/add | solution.py:313
  63.4 1.5 %collective-permute-start.1 = (bf16[8,24,1024]{2,1,0:T(8,128)(2,1)S(1)}, bf16[8,24,1024]{2,1,0:T(8,128)(2,1)}, u32[]{:S(2)}, u32[]{:S(2)}) collective-permute-start(bf16[8,24,1024]{2,1,0:T(8,128)(2,1)S(1)} %slice.110), channel_id=1, source_target_pairs={{0,2},{1,3},{2,0},{3,1},{4,6},{5,7},{6,4},{7,5},{8,10},{9,11},{10,... | collective-permute-start | bytes 1179656 | tf_op jit(solution)/shard_map/ppermute | solution.py:183
  65.0 1.5 %convert_add_fusion = f32[16,24,1024]{2,1,0:T(8,128)S(1)} fusion(f32[16,24,1024]{2,1,0:T(8,128)S(1)} %get-tuple-element.34, bf16[16,24,1024]{2,1,0:T(8,128)(2,1)} %collective-permute-done.3), kind=kLoop, calls=%fused_computation | loop fusion | flops 786432 | bytes 3932160 | tf_op jit(solution)/shard_map/add | solution.py:313
  66.6 1.5 %collective-permute-start.4 = (bf16[8,24,1024]{2,1,0:T(8,128)(2,1)S(1)}, bf16[8,24,1024]{2,1,0:T(8,128)(2,1)}, u32[]{:S(2)}, u32[]{:S(2)}) collective-permute-start(bf16[8,24,1024]{2,1,0:T(8,128)(2,1)S(1)} %slice.109), channel_id=1, source_target_pairs={{0,4},{1,5},{2,6},{3,7},{4,0},{5,1},{6,2},{7,3},{8,12},{9,13},{10,... | collective-permute-start | bytes 1179656 | tf_op jit(solution)/shard_map/ppermute | solution.py:183
  68.1 3.8 %back.1 = (bf16[1024,768]{1,0:T(8,128)(2,1)S(1)}, bf16[32,120,128]{2,1,0:T(8,128)(2,1)}) custom-call(bf16[1024,1024]{1,0:T(8,128)(2,1)S(1)} %copy-done.17, bf16[768,1024]{1,0:T(8,128)(2,1)S(1)} %copy-done.9, f32[1024,128]{1,0:T(8,128)S(1)} %copy-done.26, bf16[640,1024]{1,0:T(8,128)(2,1)S(1)} %copy-done.30), custom_call_target="tpu_custom_call" | custom-call | flops 3000000000 | bytes 8388608 | tf_op jit(solution)/shard_map/back/pallas_call | solution.py:324
  72.0 2.8 %all-to-all-start.1 = ((bf16[32,120,128]{2,1,0:T(8,128)(2,1)}), bf16[32,120,128]{2,1,0:T(8,128)(2,1)S(1)}, u32[]{:S(2)}, u32[]{:S(2)}) async-start(bf16[32,120,128]{2,1,0:T(8,128)(2,1)} %get-tuple-element.30), calls=%async_computation.1 | async-start | bytes 1966080 | tf_op jit(solution)/shard_map/all_to_all | solution.py:333
  74.8 1.5 %slice_add_fusion.1 = f32[8,24,1024]{2,1,0:T(8,128)S(1)} fusion(f32[16,24,1024]{2,1,0:T(8,128)} %copy-done.31, bf16[8,24,1024]{2,1,0:T(8,128)(2,1)} %collective-permute-done.1), kind=kLoop, calls=%fused_computation.9 | loop fusion | flops 393216 | bytes 1966080 | tf_op jit(solution)/shard_map/add | solution.py:314
  76.3 1.5 %collective-permute-start.2 = (bf16[4,24,1024]{2,1,0:T(8,128)(2,1)S(1)}, bf16[4,24,1024]{2,1,0:T(8,128)(2,1)S(1)}, u32[]{:S(2)}, u32[]{:S(2)}) collective-permute-start(bf16[4,24,1024]{2,1,0:T(8,128)(2,1)S(1)} %slice.112), channel_id=1, source_target_pairs={{0,4},{1,5},{2,6},{3,7},{4,0},{5,1},{6,2},{7,3},{8,12},{9,13},{10,... | collective-permute-start | bytes 589832 | tf_op jit(solution)/shard_map/ppermute | solution.py:183
  77.8 1.2 %collective-permute-done.4 = bf16[8,24,1024]{2,1,0:T(8,128)(2,1)} collective-permute-done((bf16[8,24,1024]{2,1,0:T(8,128)(2,1)S(1)}, bf16[8,24,1024]{2,1,0:T(8,128)(2,1)}, u32[]{:S(2)}, u32[]{:S(2)}) %collective-permute-start.4) | collective-permute-done | bytes 393248 | tf_op jit(solution)/shard_map/ppermute | solution.py:183
  79.1 1.3 %slice_add_fusion = f32[8,24,1024]{2,1,0:T(8,128)S(1)} fusion(f32[16,24,1024]{2,1,0:T(8,128)S(1)} %copy-done.33, bf16[8,24,1024]{2,1,0:T(8,128)(2,1)} %collective-permute-done.4), kind=kLoop, calls=%fused_computation.7 | loop fusion | flops 393216 | bytes 1966080 | tf_op jit(solution)/shard_map/add | solution.py:314
  80.4 2.4 %collective-permute-start.5 = (bf16[4,24,1024]{2,1,0:T(8,128)(2,1)S(1)}, bf16[4,24,1024]{2,1,0:T(8,128)(2,1)S(1)}, u32[]{:S(2)}, u32[]{:S(2)}) collective-permute-start(bf16[4,24,1024]{2,1,0:T(8,128)(2,1)S(1)} %slice.111), channel_id=1, source_target_pairs={{0,2},{1,3},{2,0},{3,1},{4,6},{5,7},{6,4},{7,5},{8,10},{9,11},{10,... | collective-permute-start | bytes 589832 | tf_op jit(solution)/shard_map/ppermute | solution.py:183
  82.8 6.3 %collective-permute-done.2 = bf16[4,24,1024]{2,1,0:T(8,128)(2,1)S(1)} collective-permute-done((bf16[4,24,1024]{2,1,0:T(8,128)(2,1)S(1)}, bf16[4,24,1024]{2,1,0:T(8,128)(2,1)S(1)}, u32[]{:S(2)}, u32[]{:S(2)}) %collective-permute-start.2) | collective-permute-done | bytes 196640 | tf_op jit(solution)/shard_map/ppermute | solution.py:183
  89.1 1.3 %collective-permute-done.5 = bf16[4,24,1024]{2,1,0:T(8,128)(2,1)S(1)} collective-permute-done((bf16[4,24,1024]{2,1,0:T(8,128)(2,1)S(1)}, bf16[4,24,1024]{2,1,0:T(8,128)(2,1)S(1)}, u32[]{:S(2)}, u32[]{:S(2)}) %collective-permute-start.5) | collective-permute-done | bytes 196640 | tf_op jit(solution)/shard_map/ppermute | solution.py:183
  90.5 1.2 %collective-permute-start.6 = (bf16[2,24,1024]{2,1,0:T(8,128)(2,1)S(1)}, bf16[2,24,1024]{2,1,0:T(8,128)(2,1)S(1)}, u32[]{:S(2)}, u32[]{:S(2)}) collective-permute-start(bf16[2,24,1024]{2,1,0:T(8,128)(2,1)S(1)} %get-tuple-element.36), channel_id=1, source_target_pairs={{0,8},{1,9},{2,10},{3,11},{4,12},{5,13},{6,14},{7,15},{8,0},{9,1},... | collective-permute-start | bytes 294920 | tf_op jit(solution)/shard_map/ppermute | solution.py:183
  91.8 1.9 %collective-permute-start.8 = (bf16[2,24,1024]{2,1,0:T(8,128)(2,1)S(1)}, bf16[2,24,1024]{2,1,0:T(8,128)(2,1)S(1)}, u32[]{:S(2)}, u32[]{:S(2)}) collective-permute-start(bf16[2,24,1024]{2,1,0:T(8,128)(2,1)S(1)} %get-tuple-element.37), channel_id=1, source_target_pairs={{0,24},{1,25},{2,26},{3,27},{4,28},{5,29},{6,30},{7,31},{8,16},{9,... | collective-permute-start | bytes 294920 | tf_op jit(solution)/shard_map/ppermute | solution.py:183
  94.2 3.4 %own.1.own_ref = f32[1024,768]{1,0:T(8,128)S(1)} custom-call(bf16[1024,1024]{1,0:T(8,128)(2,1)S(1)} %copy-done.18, bf16[768,1024]{1,0:T(8,128)(2,1)S(1)} %copy-done.11, bf16[1024,1024]{1,0:T(8,128)(2,1)S(1)} %copy-done.15, bf16[1024,768]{1,0:T(8,128)(2,1)S(1)} %get-tuple-element.29.gs_ref), custom_call_target="tpu_custom_call" | custom-call | flops 3000000000 | bytes 10485760 | tf_op jit(solution)/shard_map/own/pallas_call | solution.py:335
  97.6 1.7 %copy-done = f32[1024,768]{1,0:T(8,128)} copy-done((f32[1024,768]{1,0:T(8,128)}, f32[1024,768]{1,0:T(8,128)S(1)}, u32[]{:S(2)}) %copy-start) | copy-done | bytes 3145752
  99.3 0.6 collective-permute-done.8
  99.9 7.9 %collective-permute-done.7 = bf16[2,24,1024]{2,1,0:T(8,128)(2,1)S(1)} collective-permute-done((bf16[2,24,1024]{2,1,0:T(8,128)(2,1)S(1)}, bf16[2,24,1024]{2,1,0:T(8,128)(2,1)S(1)}, u32[]{:S(2)}, u32[]{:S(2)}) %collective-permute-start.7) | collective-permute-done | bytes 98336 | tf_op jit(solution)/shard_map/ppermute | solution.py:183
  107.9 0.7 slice_bitcast_fusion
  108.6 1.9 %copy-done.1 = f32[1024,768]{1,0:T(8,128)S(1)} copy-done((f32[1024,768]{1,0:T(8,128)S(1)}, f32[1024,768]{1,0:T(8,128)}, u32[]{:S(2)}) %copy-start.1) | copy-done | bytes 3145752
  110.5 3.3 %final.1 = f32[1024,768]{1,0:T(8,128)} custom-call(s32[1,4]{1,0:T(1,128)S(1)} %copy-done.2, f32[1024,768]{1,0:T(8,128)S(1)} %copy-done.1, bf16[32,120,128]{2,1,0:T(8,128)(2,1)S(1)} %all-to-all-done.1.got_ref, s32[1,512]{1,0:T(1,128)S(1)} %broadcast_select_fusion.idx_ref), custom_call_target="tpu_custom_call" | custom-call | flops 1000000000 | bytes 8388608 | tf_op jit(solution)/shard_map/final/pallas_call | solution.py:345
  (74 shorter events, 1.4 us)
Async XLA Ops:
  3.3 1.4 %copy-start.5 = (bf16[1024,768]{1,0:T(8,128)(2,1)S(1)}, bf16[1024,768]{1,0:T(8,128)(2,1)}, u32[]{:S(2)}) copy-start(bf16[1024,768]{1,0:T(8,128)(2,1)} %x_ref.1) | copy-start | bytes 4718596
  4.7 9.5 %copy-start.3 = (bf16[8,8,128,128]{3,2,1,0:T(8,128)(2,1)S(1)}, bf16[8,8,128,128]{3,2,1,0:T(8,128)(2,1)}, u32[]{:S(2)}) copy-start(bf16[8,8,128,128]{3,2,1,0:T(8,128)(2,1)} %tiles_ref.1) | copy-start | bytes 6291460
  6.9 7.3 %copy-start.12 = (s32[8,8]{1,0:T(8,128)S(1)}, s32[8,8]{1,0:T(8,128)}, u32[]{:S(2)}) copy-start(s32[8,8]{1,0:T(8,128)} %src_ref.1) | copy-start | bytes 772
  6.9 7.3 %copy-start.13 = (s32[8]{0:T(128)S(1)}, s32[8]{0:T(128)}, u32[]{:S(2)}) copy-start(s32[8]{0:T(128)} %count_ref.1) | copy-start | bytes 100
  6.9 32.1 %all-to-all-start = ((bf16[32,120,128]{2,1,0:T(8,128)(2,1)}), bf16[32,120,128]{2,1,0:T(8,128)(2,1)S(1)}, u32[]{:S(2)}, u32[]{:S(2)}) async-start(bf16[32,120,128]{2,1,0:T(8,128)(2,1)} %pack.1), calls=%async_computation | async-start | bytes 1966080 | tf_op jit(solution)/shard_map/all_to_all | solution.py:229
  14.2 1.4 %copy-start.6 = (bf16[1024,768]{1,0:T(8,128)(2,1)S(1)}, bf16[1024,768]{1,0:T(8,128)(2,1)}, u32[]{:S(2)}) copy-start(bf16[1024,768]{1,0:T(8,128)(2,1)} %x_ref.1) | copy-start | bytes 4718596
  15.6 1.4 %copy-start.10 = (bf16[768,1024]{1,0:T(8,128)(2,1)S(1)}, bf16[768,1024]{1,0:T(8,128)(2,1)}, u32[]{:S(2)}) copy-start(bf16[768,1024]{1,0:T(8,128)(2,1)} %w_ref.7) | copy-start | bytes 4718596
  24.3 1.4 %copy-start.14 = (bf16[1024,1024]{1,0:T(8,128)(2,1)}, bf16[1024,1024]{1,0:T(8,128)(2,1)S(1)}, u32[]{:S(2)}) copy-start(bf16[1024,1024]{1,0:T(8,128)(2,1)S(1)} %get-tuple-element.26.own_t_ref) | copy-start | bytes 6291460
  25.7 2.0 %copy-start.19 = (f32[1024,1024]{1,0:T(8,128)}, f32[1024,1024]{1,0:T(8,128)S(1)}, u32[]{:S(2)}) copy-start(f32[1024,1024]{1,0:T(8,128)S(1)} %get-tuple-element.23.pre_ref) | copy-start | bytes 12582916
  27.7 1.7 %copy-start.21 = (f32[1024,768]{1,0:T(8,128)}, f32[1024,768]{1,0:T(8,128)S(1)}, u32[]{:S(2)}) copy-start(f32[1024,768]{1,0:T(8,128)S(1)} %get-tuple-element.21.numer_ref) | copy-start | bytes 9437188
  29.3 1.1 copy-start.23
  30.4 0.8 copy-start.27
  31.2 1.1 copy-start.29
  39.0 1.6 %copy-start.4 = (bf16[1024,1024]{1,0:T(8,128)(2,1)S(1)}, bf16[1024,1024]{1,0:T(8,128)(2,1)}, u32[]{:S(2)}) copy-start(bf16[1024,1024]{1,0:T(8,128)(2,1)} %cot_ref.1) | copy-start | bytes 6291460
  40.6 1.4 %copy-start.8 = (bf16[768,1024]{1,0:T(8,128)(2,1)S(1)}, bf16[768,1024]{1,0:T(8,128)(2,1)}, u32[]{:S(2)}) copy-start(bf16[768,1024]{1,0:T(8,128)(2,1)} %w_ref.6) | copy-start | bytes 4718596
  42.0 2.2 %copy-start.20 = (f32[1024,1024]{1,0:T(8,128)S(1)}, f32[1024,1024]{1,0:T(8,128)}, u32[]{:S(2)}) copy-start(f32[1024,1024]{1,0:T(8,128)} %copy-done.19) | copy-start | bytes 12582916
  44.2 1.9 %copy-start.22 = (f32[1024,768]{1,0:T(8,128)S(1)}, f32[1024,768]{1,0:T(8,128)}, u32[]{:S(2)}) copy-start(f32[1024,768]{1,0:T(8,128)} %copy-done.21) | copy-start | bytes 9437188
  46.1 1.3 %copy-start.24 = (bf16[1024,640]{1,0:T(8,128)(2,1)S(1)}, bf16[1024,640]{1,0:T(8,128)(2,1)}, u32[]{:S(2)}) copy-start(bf16[1024,640]{1,0:T(8,128)(2,1)} %copy-done.23) | copy-start | bytes 3932164
  47.4 1.0 copy-start.28
  48.5 7.0 %copy-start.7 = (bf16[1024,768]{1,0:T(8,128)(2,1)S(1)}, bf16[1024,768]{1,0:T(8,128)(2,1)}, u32[]{:S(2)}) copy-start(bf16[1024,768]{1,0:T(8,128)(2,1)} %x_ref.1) | copy-start | bytes 4718596
  55.5 2.9 %copy-start.25 = (f32[1024,128]{1,0:T(8,128)}, f32[1024,128]{1,0:T(8,128)S(1)}, u32[]{:S(2)}) copy-start(f32[1024,128]{1,0:T(8,128)S(1)} %get-tuple-element.27.inv_ref) | copy-start | bytes 1572868
  55.5 2.9 %copy-start.16 = (bf16[1024,1024]{1,0:T(8,128)(2,1)}, bf16[1024,1024]{1,0:T(8,128)(2,1)S(1)}, u32[]{:S(2)}) copy-start(bf16[1024,1024]{1,0:T(8,128)(2,1)S(1)} %get-tuple-element.25.gp_ref) | copy-start | bytes 6291460
  58.4 3.6 %collective-permute-start = (bf16[16,24,1024]{2,1,0:T(8,128)(2,1)}, bf16[16,24,1024]{2,1,0:T(8,128)(2,1)}, u32[]{:S(2)}, u32[]{:S(2)}) collective-permute-start(bf16[16,24,1024]{2,1,0:T(8,128)(2,1)} %get-tuple-element.32), channel_id=1, source_target_pairs={{0,1},{1,0},{2,3},{3,2},{4,5},{5,4},{6,7},{7,6},{8,9},{9,8},{10,11... | collective-permute-start | bytes 2359304 | tf_op jit(solution)/shard_map/ppermute | solution.py:183
  61.3 3.7 %collective-permute-start.3 = (bf16[16,24,1024]{2,1,0:T(8,128)(2,1)}, bf16[16,24,1024]{2,1,0:T(8,128)(2,1)}, u32[]{:S(2)}, u32[]{:S(2)}) collective-permute-start(bf16[16,24,1024]{2,1,0:T(8,128)(2,1)} %get-tuple-element.35), channel_id=1, source_target_pairs={{0,1},{1,0},{2,3},{3,2},{4,5},{5,4},{6,7},{7,6},{8,9},{9,8},{10,11... | collective-permute-start | bytes 2359304 | tf_op jit(solution)/shard_map/ppermute | solution.py:183
  63.3 3.1 %copy-start.31 = (f32[16,24,1024]{2,1,0:T(8,128)}, f32[16,24,1024]{2,1,0:T(8,128)S(1)}, u32[]{:S(2)}) copy-start(f32[16,24,1024]{2,1,0:T(8,128)S(1)} %convert_add_fusion.1) | copy-start | bytes 4718596
  63.4 4.7 %copy-start.30 = (bf16[640,1024]{1,0:T(8,128)(2,1)S(1)}, bf16[640,1024]{1,0:T(8,128)(2,1)}, u32[]{:S(2)}) copy-start(bf16[640,1024]{1,0:T(8,128)(2,1)} %copy-done.29) | copy-start | bytes 3932164
  63.4 11.4 %collective-permute-start.1 = (bf16[8,24,1024]{2,1,0:T(8,128)(2,1)S(1)}, bf16[8,24,1024]{2,1,0:T(8,128)(2,1)}, u32[]{:S(2)}, u32[]{:S(2)}) collective-permute-start(bf16[8,24,1024]{2,1,0:T(8,128)(2,1)S(1)} %slice.110), channel_id=1, source_target_pairs={{0,2},{1,3},{2,0},{3,1},{4,6},{5,7},{6,4},{7,5},{8,10},{9,11},{10,... | collective-permute-start | bytes 1179656 | tf_op jit(solution)/shard_map/ppermute | solution.py:183
  65.0 3.1 %copy-start.9 = (bf16[768,1024]{1,0:T(8,128)(2,1)S(1)}, bf16[768,1024]{1,0:T(8,128)(2,1)}, u32[]{:S(2)}) copy-start(bf16[768,1024]{1,0:T(8,128)(2,1)} %w_ref.6) | copy-start | bytes 4718596
  65.0 3.1 %copy-start.17 = (bf16[1024,1024]{1,0:T(8,128)(2,1)S(1)}, bf16[1024,1024]{1,0:T(8,128)(2,1)}, u32[]{:S(2)}) copy-start(bf16[1024,1024]{1,0:T(8,128)(2,1)} %copy-done.16) | copy-start | bytes 6291460
  65.0 3.1 %copy-start.26 = (f32[1024,128]{1,0:T(8,128)S(1)}, f32[1024,128]{1,0:T(8,128)}, u32[]{:S(2)}) copy-start(f32[1024,128]{1,0:T(8,128)} %copy-done.25) | copy-start | bytes 1572868
  66.5 1.6 %copy-start.32 = (f32[16,24,1024]{2,1,0:T(8,128)}, f32[16,24,1024]{2,1,0:T(8,128)S(1)}, u32[]{:S(2)}) copy-start(f32[16,24,1024]{2,1,0:T(8,128)S(1)} %convert_add_fusion) | copy-start | bytes 4718596
  66.6 12.5 %collective-permute-start.4 = (bf16[8,24,1024]{2,1,0:T(8,128)(2,1)S(1)}, bf16[8,24,1024]{2,1,0:T(8,128)(2,1)}, u32[]{:S(2)}, u32[]{:S(2)}) collective-permute-start(bf16[8,24,1024]{2,1,0:T(8,128)(2,1)S(1)} %slice.109), channel_id=1, source_target_pairs={{0,4},{1,5},{2,6},{3,7},{4,0},{5,1},{6,2},{7,3},{8,12},{9,13},{10,... | collective-permute-start | bytes 1179656 | tf_op jit(solution)/shard_map/ppermute | solution.py:183
  72.0 36.6 %all-to-all-start.1 = ((bf16[32,120,128]{2,1,0:T(8,128)(2,1)}), bf16[32,120,128]{2,1,0:T(8,128)(2,1)S(1)}, u32[]{:S(2)}, u32[]{:S(2)}) async-start(bf16[32,120,128]{2,1,0:T(8,128)(2,1)} %get-tuple-element.30), calls=%async_computation.1 | async-start | bytes 1966080 | tf_op jit(solution)/shard_map/all_to_all | solution.py:333
  74.8 4.3 %copy-start.33 = (f32[16,24,1024]{2,1,0:T(8,128)S(1)}, f32[16,24,1024]{2,1,0:T(8,128)}, u32[]{:S(2)}) copy-start(f32[16,24,1024]{2,1,0:T(8,128)} %copy-done.32) | copy-start | bytes 4718596
  76.3 12.8 %collective-permute-start.2 = (bf16[4,24,1024]{2,1,0:T(8,128)(2,1)S(1)}, bf16[4,24,1024]{2,1,0:T(8,128)(2,1)S(1)}, u32[]{:S(2)}, u32[]{:S(2)}) collective-permute-start(bf16[4,24,1024]{2,1,0:T(8,128)(2,1)S(1)} %slice.112), channel_id=1, source_target_pairs={{0,4},{1,5},{2,6},{3,7},{4,0},{5,1},{6,2},{7,3},{8,12},{9,13},{10,... | collective-permute-start | bytes 589832 | tf_op jit(solution)/shard_map/ppermute | solution.py:183
  79.1 15.1 %copy-start.18 = (bf16[1024,1024]{1,0:T(8,128)(2,1)S(1)}, bf16[1024,1024]{1,0:T(8,128)(2,1)}, u32[]{:S(2)}) copy-start(bf16[1024,1024]{1,0:T(8,128)(2,1)} %copy-done.16) | copy-start | bytes 6291460
  80.4 10.0 %collective-permute-start.5 = (bf16[4,24,1024]{2,1,0:T(8,128)(2,1)S(1)}, bf16[4,24,1024]{2,1,0:T(8,128)(2,1)S(1)}, u32[]{:S(2)}, u32[]{:S(2)}) collective-permute-start(bf16[4,24,1024]{2,1,0:T(8,128)(2,1)S(1)} %slice.111), channel_id=1, source_target_pairs={{0,2},{1,3},{2,0},{3,1},{4,6},{5,7},{6,4},{7,5},{8,10},{9,11},{10,... | collective-permute-start | bytes 589832 | tf_op jit(solution)/shard_map/ppermute | solution.py:183
  89.1 5.1 %copy-start.15 = (bf16[1024,1024]{1,0:T(8,128)(2,1)S(1)}, bf16[1024,1024]{1,0:T(8,128)(2,1)}, u32[]{:S(2)}) copy-start(bf16[1024,1024]{1,0:T(8,128)(2,1)} %copy-done.14) | copy-start | bytes 6291460
  89.1 5.1 %copy-start.11 = (bf16[768,1024]{1,0:T(8,128)(2,1)S(1)}, bf16[768,1024]{1,0:T(8,128)(2,1)}, u32[]{:S(2)}) copy-start(bf16[768,1024]{1,0:T(8,128)(2,1)} %w_ref.7) | copy-start | bytes 4718596
  90.5 8.8 %collective-permute-start.6 = (bf16[2,24,1024]{2,1,0:T(8,128)(2,1)S(1)}, bf16[2,24,1024]{2,1,0:T(8,128)(2,1)S(1)}, u32[]{:S(2)}, u32[]{:S(2)}) collective-permute-start(bf16[2,24,1024]{2,1,0:T(8,128)(2,1)S(1)} %get-tuple-element.36), channel_id=1, source_target_pairs={{0,8},{1,9},{2,10},{3,11},{4,12},{5,13},{6,14},{7,15},{8,0},{9,1},... | collective-permute-start | bytes 294920 | tf_op jit(solution)/shard_map/ppermute | solution.py:183
  91.8 8.1 %collective-permute-start.8 = (bf16[2,24,1024]{2,1,0:T(8,128)(2,1)S(1)}, bf16[2,24,1024]{2,1,0:T(8,128)(2,1)S(1)}, u32[]{:S(2)}, u32[]{:S(2)}) collective-permute-start(bf16[2,24,1024]{2,1,0:T(8,128)(2,1)S(1)} %get-tuple-element.37), channel_id=1, source_target_pairs={{0,24},{1,25},{2,26},{3,27},{4,28},{5,29},{6,30},{7,31},{8,16},{9,... | collective-permute-start | bytes 294920 | tf_op jit(solution)/shard_map/ppermute | solution.py:183
  93.7 14.1 %collective-permute-start.7 = (bf16[2,24,1024]{2,1,0:T(8,128)(2,1)S(1)}, bf16[2,24,1024]{2,1,0:T(8,128)(2,1)S(1)}, u32[]{:S(2)}, u32[]{:S(2)}) collective-permute-start(bf16[2,24,1024]{2,1,0:T(8,128)(2,1)S(1)} %get-tuple-element.38), channel_id=1, source_target_pairs={{0,16},{1,17},{2,18},{3,19},{4,20},{5,21},{6,22},{7,23},{8,24},{9,... | collective-permute-start | bytes 294920 | tf_op jit(solution)/shard_map/ppermute | solution.py:183
  97.6 1.7 %copy-start = (f32[1024,768]{1,0:T(8,128)}, f32[1024,768]{1,0:T(8,128)S(1)}, u32[]{:S(2)}) copy-start(f32[1024,768]{1,0:T(8,128)S(1)} %own.1.own_ref) | copy-start | bytes 9437188
  99.3 9.3 %copy-start.2 = (s32[1,4]{1,0:T(1,128)S(1)}, s32[1,4]{1,0:T(1,128)}, u32[]{:S(2)}) copy-start(s32[1,4]{1,0:T(1,128)} %hub_ref.1) | copy-start | bytes 52
  108.6 1.9 %copy-start.1 = (f32[1024,768]{1,0:T(8,128)S(1)}, f32[1024,768]{1,0:T(8,128)}, u32[]{:S(2)}) copy-start(f32[1024,768]{1,0:T(8,128)} %copy-done) | copy-start | bytes 9437188

commit v2 on v0

--- a/solution.py
+++ b/solution.py
@@ -1,7 +1,484 @@
+import functools
+
 import jax
 import jax.numpy as jnp
 from jax import lax
+from jax.experimental import pallas as pl
+from jax.experimental.pallas import tpu as pltpu
 from jax.sharding import PartitionSpec as P
+
+BF16 = jnp.bfloat16
+F32 = jnp.float32
+LANES = 128
+MIB = 1 << 20
+LIMIT = 58
+
+
+def mm(a, b, contract=((1,), (0,))):
+    return lax.dot_general(a, b, (contract, ((), ())), preferred_element_type=F32)
+
+
+def params(mib):
+    return pltpu.CompilerParams(vmem_limit_bytes=mib * MIB)
+
+
+def cost(flops, moved):
+    return pl.CostEstimate(flops=flops, bytes_accessed=moved, transcendentals=0)
+
+
+def slot_indices(send_ref, count_ref):
+    sub = lax.broadcasted_iota(jnp.int32, send_ref.shape, 0)
+    return jnp.where(sub < count_ref[...], send_ref[...], -1)
+
+
+def pack_kernel(send_ref, count_ref, hub_ref, feat_ref, out_ref, hits):
+    caps, parts = send_ref.shape
+    rows, width = feat_ref.shape
+    bnd = parts * caps
+    groups = width // LANES
+    idx = slot_indices(send_ref, count_ref)
+    lane = lax.broadcasted_iota(jnp.int32, (caps, rows), 1)
+    for d in range(parts):
+        hit = jnp.where(lane == idx[:, d : d + 1], 1.0, 0.0)
+        hits[d * caps : (d + 1) * caps, :] = hit.astype(BF16)
+    sub = lax.broadcasted_iota(jnp.int32, (16, rows), 0) % 4
+    lane = lax.broadcasted_iota(jnp.int32, (16, rows), 1)
+    hub = jnp.zeros((16, rows), F32)
+    for i in range(4):
+        hub = jnp.where((sub == i) & (lane == hub_ref[0, i]), 1.0, hub)
+    hits[bnd:, :] = hub.astype(BF16)
+    picked = mm(hits[...], feat_ref[...])
+    for d in range(parts):
+        piece = picked[d * caps : (d + 1) * caps]
+        piece = jnp.where(idx[:, d : d + 1] >= 0, piece, jnp.inf).astype(BF16)
+        for g in range(groups):
+            out_ref[d, g * caps : (g + 1) * caps, :] = piece[:, g * LANES : (g + 1) * LANES]
+    hubs = picked[bnd : bnd + 8]
+    low = lax.broadcasted_iota(jnp.int32, (8, LANES), 0) < 4
+    block = []
+    for j in range(groups // 2):
+        left = hubs[:, 2 * j * LANES : (2 * j + 1) * LANES]
+        right = hubs[:, (2 * j + 1) * LANES : (2 * j + 2) * LANES]
+        block.append(jnp.where(low, left, right))
+    block = jnp.concatenate(block, axis=0).astype(BF16)
+    out_ref[:, groups * caps :, :] = jnp.broadcast_to(block[None], (parts, groups * 4, LANES))
+
+
+def early_kernel(src_ref, count_ref, tiles_ref, feat_ref, *rest):
+    bnd_ref, own_t_ref, numer_ref, degree_ref, acc = rest
+    step = pl.program_id(0)
+    here, slots, tile, _ = tiles_ref.shape
+    own = own_t_ref.shape[0]
+    acc[...] = jnp.zeros_like(acc)
+    for t in range(here):
+        block = step * here + t
+        for k in range(slots):
+
+            @pl.when(k < count_ref[block])
+            def _():
+                at = pl.ds(pl.multiple_of(src_ref[block, k] * tile, tile), tile)
+                acc[t * tile : (t + 1) * tile, at] += tiles_ref[t, k].astype(F32)
+
+    dense = acc[...].astype(BF16)
+    bnd_ref[...] = dense[:, own:]
+    own_t_ref[...] = dense[:, :own].T
+    numer_ref[...] = mm(dense[:, :own], feat_ref[...])
+    degree_ref[...] = mm(dense[:, :own], jnp.ones((own, LANES), BF16))
+
+
+def unpack_table(caps, got_ref, table):
+    parts = got_ref.shape[0]
+    bnd = parts * caps
+    width = table.shape[1] - LANES
+    groups = width // LANES
+    for g in range(groups):
+        piece = got_ref[:, g * caps : (g + 1) * caps, :].astype(F32).reshape(bnd, LANES)
+        used = piece < jnp.inf
+        table[:bnd, g * LANES : (g + 1) * LANES] = jnp.where(used, piece, 0.0).astype(BF16)
+        if g == 0:
+            table[:bnd, width:] = jnp.where(used, 1.0, 0.0).astype(BF16)
+    hub_rows = groups * 4
+    hubs = got_ref[:, groups * caps :, :].astype(F32).reshape(parts * hub_rows, LANES)
+    down = pltpu.roll(hubs, 4, 0).reshape(parts // 2, 2 * hub_rows, LANES)
+    up = pltpu.roll(hubs, parts * hub_rows - 4, 0).reshape(parts // 2, 2 * hub_rows, LANES)
+    hubs = hubs.reshape(parts // 2, 2 * hub_rows, LANES)
+    low = lax.broadcasted_iota(jnp.int32, (parts // 2, hub_rows, LANES), 1) % 8 < 4
+    even = jnp.where(low, hubs[:, :hub_rows], down[:, hub_rows:]).astype(BF16)
+    odd = jnp.where(low, up[:, :hub_rows], hubs[:, hub_rows:]).astype(BF16)
+    for g in range(groups):
+        half = even if g % 2 == 0 else odd
+        j = g // 2
+        piece = half[:, 8 * j : 8 * j + 8, :].reshape(parts * 4, LANES)
+        table[bnd:, g * LANES : (g + 1) * LANES] = piece
+    table[bnd:, width:] = jnp.ones((parts * 4, LANES), BF16)
+
+
+def pack_grads(caps, grads, out_ref):
+    parts = out_ref.shape[0]
+    bnd = parts * caps
+    groups = grads.shape[1] // LANES
+    for g in range(groups):
+        piece = grads[:bnd, g * LANES : (g + 1) * LANES].astype(BF16)
+        out_ref[:, g * caps : (g + 1) * caps, :] = piece.reshape(parts, caps, LANES)
+    half = parts // 2
+    low = lax.broadcasted_iota(jnp.int32, (half, 8, LANES), 1) < 4
+    even, odd = [], []
+    for j in range(groups // 2):
+        a = grads[bnd:, 2 * j * LANES : (2 * j + 1) * LANES]
+        b = grads[bnd:, (2 * j + 1) * LANES : (2 * j + 2) * LANES]
+        up = pltpu.roll(a, parts * 4 - 4, 0).reshape(half, 8, LANES)
+        down = pltpu.roll(b, 4, 0).reshape(half, 8, LANES)
+        a, b = a.reshape(half, 8, LANES), b.reshape(half, 8, LANES)
+        even.append(jnp.where(low, a, down))
+        odd.append(jnp.where(low, up, b))
+    hubs = jnp.concatenate(even + odd, axis=1).reshape(parts, groups * 4, LANES)
+    out_ref[:, groups * caps :, :] = hubs.astype(BF16)
+
+
+def main_kernel(caps, masks, *refs):
+    outs_hbm, held, outs_all = refs[8:16], refs[16:24], refs[24:32]
+    table, pre_all, agg_all, acc, in_sem, out_sem, chain_sem, back_sem = refs[32:]
+    out_hbm, gp_hbm, gs_hbm, *chain_hbm, back_hbm = outs_hbm
+    out_all, gp_all, gs_all, *chain_all, back_all = outs_all
+    got, bnd, numer, degree, feat, cot, wn, ws = held
+    width = numer.shape[1]
+    loads = [
+        pltpu.make_async_copy(a, b, in_sem.at[i]) for i, (a, b) in enumerate(zip(refs[:8], held))
+    ]
+    for i in (7, 4, 0, 1, 3, 2, 6, 5):
+        loads[i].start()
+    for i in (7, 4):
+        loads[i].wait()
+    pre_all[...] = mm(feat[...], ws[...])
+    loads[0].wait()
+    unpack_table(caps, got, table)
+    for i in (1, 2, 3):
+        loads[i].wait()
+    num = numer[...] + mm(bnd[...], table[:, :width])
+    inv = 1.0 / (degree[...] + mm(bnd[...], table[:, width:]))
+    degree[...] = inv
+    agg = (num * jnp.concatenate([inv] * (width // LANES), axis=1)).astype(BF16)
+    agg_all[...] = agg
+    loads[6].wait()
+    pre = pre_all[...] + mm(agg_all[...], wn[...])
+    loads[5].wait()
+    sig = 0.5 * jnp.tanh(0.5 * pre) + 0.5
+    out = pre * sig
+    out_all[...] = out.astype(BF16)
+    gp_all[...] = (cot[...].astype(F32) * (sig + out * (1.0 - sig))).astype(BF16)
+    stores = [pltpu.make_async_copy(out_all, out_hbm, out_sem.at[0])]
+    stores.append(pltpu.make_async_copy(gp_all, gp_hbm, out_sem.at[1]))
+    for store in stores:
+        store.start()
+    inv = jnp.concatenate([degree[...]] * (width // LANES), axis=1)
+    gs_all[...] = (mm(gp_all[...], wn[...], ((1,), (1,))) * inv).astype(BF16)
+    stores.append(pltpu.make_async_copy(gs_all, gs_hbm, out_sem.at[2]))
+    stores[-1].start()
+    me = lax.axis_index("dom")
+    *keeps, send = chain_all
+    share = send.shape[2]
+    places = [(ref, p) for ref in keeps for p in range(ref.shape[1])]
+    for chain, x in enumerate((agg_all, feat)):
+        acc[...] = mm(x[...], gp_all[...], ((0,), (0,)))
+        for p, mask in enumerate(masks[chain]):
+            mine = jnp.bitwise_xor(me, mask)
+            other = jnp.bitwise_xor(me, mask + 1)
+            keep, at = places[p]
+            keep[chain, at] = acc[pl.ds(pl.multiple_of(mine * share, 8), share), :]
+            send[chain, p] = acc[pl.ds(pl.multiple_of(other * share, 8), share), :].astype(BF16)
+        for i, (a, b) in enumerate(zip(chain_all, chain_hbm)):
+            stores.append(pltpu.make_async_copy(a.at[chain], b.at[chain], chain_sem.at[chain, i]))
+            stores[-1].start()
+    pack_grads(caps, mm(bnd[...], gs_all[...], ((0,), (0,))), back_all)
+    stores.append(pltpu.make_async_copy(back_all, back_hbm, back_sem))
+    stores[-1].start()
+    for store in stores:
+        store.wait()
+
+
+def stage_one_kernel(keep_ref, core_ref, a_ref, b_ref, token_ref):
+    token_ref[...] = jnp.zeros_like(token_ref)
+    for chain, ref in ((0, a_ref), (1, b_ref)):
+        ref[...] = (keep_ref[chain] + core_ref[chain].astype(F32)).astype(BF16)
+
+
+def stage_two_kernel(keep_ref, core_ref, a1_ref, b1_ref, _, a_ref, b_ref):
+    for chain, got, ref in ((0, a1_ref, a_ref), (1, b1_ref, b_ref)):
+        total = keep_ref[chain] + core_ref[chain].astype(F32) + got[...].astype(F32)
+        ref[...] = total.astype(BF16)
+
+
+def stage_z_kernel(keep_ref, core_ref, a1_ref, b1_ref, a2_ref, b2_ref, token_ref, base_ref, *outs):
+    token_ref[...] = jnp.zeros_like(token_ref)
+    for chain, one, two in ((0, a1_ref, a2_ref), (1, b1_ref, b2_ref)):
+        total = keep_ref[chain] + core_ref[chain].astype(F32)
+        total = total + one[...].astype(F32) + two[...].astype(F32)
+        base_ref[chain] = total[0]
+        for z, ref in enumerate(outs):
+            ref[chain] = total[z + 1].astype(BF16)
+
+
+def stage_last_kernel(base_ref, z1_ref, z2_ref, z3_ref, _, neigh_ref, self_ref):
+    for chain, ref in ((0, neigh_ref), (1, self_ref)):
+        total = base_ref[chain] + z1_ref[chain].astype(F32)
+        ref[...] = total + z2_ref[chain].astype(F32) + z3_ref[chain].astype(F32)
+
+
+def own_kernel(send_ref, count_ref, gp_ref, w_ref, own_t_ref, gs_ref, _, out_ref, place_ref, token_ref, hits):
+    token_ref[...] = jnp.zeros_like(token_ref)
+    out_ref[...] = mm(gp_ref[...], w_ref[...], ((1,), (1,))) + mm(own_t_ref[...], gs_ref[...])
+    caps, parts = send_ref.shape
+    here = hits.shape[1]
+    idx = slot_indices(send_ref, count_ref) - pl.program_id(0) * here
+    lane = lax.broadcasted_iota(jnp.int32, (caps, here), 1)
+    for d in range(parts):
+        hit = jnp.where(lane == idx[:, d : d + 1], 1.0, 0.0)
+        hits[d * caps : (d + 1) * caps, :] = hit.astype(BF16)
+    place_ref[...] = hits[...].T
+
+
+def final_kernel(caps, hub_ref, own_ref, got_ref, place_ref, _, out_ref, token_ref, rows):
+    token_ref[...] = jnp.zeros_like(token_ref)
+    step = pl.program_id(0)
+    parts = got_ref.shape[0]
+    bnd = parts * caps
+    here, width = out_ref.shape
+    groups = width // LANES
+
+    @pl.when(step == 0)
+    def _():
+        for g in range(groups):
+            piece = got_ref[:, g * caps : (g + 1) * caps, :]
+            rows[:, g * LANES : (g + 1) * LANES] = piece.reshape(bnd, LANES)
+
+    out_ref[...] = own_ref[...] + mm(place_ref[...], rows[...])
+    hubs = jnp.sum(got_ref[:, groups * caps :, :].astype(F32), axis=0)
+    for i in range(4):
+        row = jnp.concatenate([hubs[4 * g + i : 4 * g + i + 1] for g in range(groups)], axis=1)
+        at = hub_ref[0, i] - step * here
+
+        @pl.when((at >= 0) & (at < here))
+        def _():
+            out_ref[pl.ds(at, 1), :] += row
+
+
+def swap(x, mask, parts):
+    return lax.ppermute(x, "dom", [(d, d ^ mask) for d in range(parts)])
+
+
+VMEM = pl.BlockSpec(memory_space=pltpu.VMEM)
+SMEM = pl.BlockSpec(memory_space=pltpu.SMEM)
+ANY = pl.BlockSpec(memory_space=pl.ANY)
+
+
+def on_device_fast(
+    features,
+    w_self,
+    w_neigh,
+    cotangent,
+    tiles,
+    tile_src,
+    tile_count,
+    send_rows,
+    send_count,
+    hub_rows,
+):
+    parts = lax.axis_size("dom")
+    rows, width = features.shape
+    hidden = w_self.shape[1]
+    blocks, slots, tile, _ = tiles.shape
+    caps = send_rows.shape[2]
+    hub_own = hub_rows.shape[1]
+    bnd = parts * caps
+    far = bnd + parts * hub_own
+    groups = width // LANES
+    sent_rows = groups * (caps + hub_own)
+    shape = jax.ShapeDtypeStruct
+
+    send_t = send_rows[0].T
+
+    outgoing = pl.pallas_call(
+        pack_kernel,
+        out_shape=shape((parts, sent_rows, LANES), BF16),
+        in_specs=[VMEM, VMEM, SMEM, VMEM],
+        out_specs=VMEM,
+        scratch_shapes=[pltpu.VMEM((bnd + 16, rows), BF16)],
+        compiler_params=params(LIMIT),
+        cost_estimate=cost(2 * bnd * rows * width, 4 * MIB),
+        name="pack",
+    )(send_t, send_count, hub_rows, features)
+    got = lax.all_to_all(outgoing, "dom", split_axis=0, concat_axis=0, tiled=True)
+
+    steps = 4
+    per = rows // steps
+    row_block = lambda n: pl.BlockSpec((per, n), lambda s: (s, 0))
+    col_block = lambda n: pl.BlockSpec((n, per), lambda s: (0, s))
+    whole = lambda *n: pl.BlockSpec(n, lambda s: (0,) * len(n))
+    bnd_adj, own_adj_t, numer, degree = pl.pallas_call(
+        early_kernel,
+        grid=(steps,),
+        out_shape=(
+            shape((rows, far), BF16),
+            shape((rows, rows), BF16),
+            shape((rows, width), F32),
+            shape((rows, LANES), F32),
+        ),
+        in_specs=[
+            SMEM,
+            SMEM,
+            pl.BlockSpec((blocks // steps, slots, tile, tile), lambda s: (s, 0, 0, 0)),
+            whole(rows, width),
+        ],
+        out_specs=(row_block(far), col_block(rows), row_block(width), row_block(LANES)),
+        scratch_shapes=[pltpu.VMEM((per, rows + far), F32)],
+        compiler_params=params(LIMIT),
+        cost_estimate=cost(6 * 10**9, 16 * MIB),
+        name="early",
+    )(tile_src, tile_count, tiles, features)
+
+    share = width // parts
+    half = parts // 2
+    order = lambda first, second: [
+        first * (p >> 3) | second * (p >> 2 & 1) | (p & 3) << 3 for p in range(half)
+    ]
+    outs = [
+        shape((rows, hidden), BF16),
+        shape((rows, hidden), BF16),
+        shape((rows, width), BF16),
+        shape((2, 4, share, hidden), F32),
+        shape((2, 4, share, hidden), F32),
+        shape((2, 8, share, hidden), F32),
+        shape((2, half, share, hidden), BF16),
+        shape((parts, sent_rows, LANES), BF16),
+    ]
+    operands = [got, bnd_adj, numer, degree, features, cotangent, w_neigh, w_self]
+    layer_out, grad_pre, gs, keep_low, keep_mid, keep_high, send, back = pl.pallas_call(
+        functools.partial(main_kernel, caps, (order(4, 2), order(2, 4))),
+        out_shape=tuple(outs),
+        in_specs=[ANY] + [ANY] * 7,
+        out_specs=(ANY,) * 8,
+        scratch_shapes=[pltpu.VMEM(a.shape, a.dtype) for a in operands + outs]
+        + [
+            pltpu.VMEM((far, width + LANES), BF16),
+            pltpu.VMEM((rows, hidden), F32),
+            pltpu.VMEM((rows, width), BF16),
+            pltpu.VMEM((width, hidden), F32),
+            pltpu.SemaphoreType.DMA((8,)),
+            pltpu.SemaphoreType.DMA((3,)),
+            pltpu.SemaphoreType.DMA((2, 4)),
+            pltpu.SemaphoreType.DMA(()),
+        ],
+        compiler_params=params(LIMIT),
+        cost_estimate=cost(10**10, 24 * MIB),
+        name="middle",
+    )(*operands)
+
+    core = swap(send, 1, parts)
+    returned = lax.all_to_all(back, "dom", split_axis=0, concat_axis=0, tiled=True)
+
+    both = lambda n, at: pl.BlockSpec((2, n, share, hidden), lambda s: (0, at, 0, 0))
+    one = lambda n, at: pl.BlockSpec((n, share, hidden), lambda s: (at, 0, 0))
+
+    def stage(kernel, name, in_specs, out_shape, out_specs, *operands):
+        return pl.pallas_call(
+            kernel,
+            grid=(1,),
+            out_shape=out_shape,
+            in_specs=in_specs,
+            out_specs=out_specs,
+            compiler_params=params(12),
+            cost_estimate=cost(10**6, 3 * MIB),
+            name=name,
+        )(*operands)
+
+    halves = shape((half // 2, share, hidden), BF16)
+    token = shape((8, LANES), F32)
+    token_at = pl.BlockSpec((8, LANES), lambda s: (0, 0))
+    a1, b1, sent_one = stage(
+        stage_one_kernel,
+        "stage_one",
+        [both(8, 0), both(8, 1)],
+        (halves, halves, token),
+        (one(8, 0), one(8, 0), token_at),
+        keep_high,
+        core,
+    )
+    got_a1, got_b1 = swap(a1, 4, parts), swap(b1, 2, parts)
+    own_grad, place, own_done = pl.pallas_call(
+        own_kernel,
+        grid=(steps,),
+        out_shape=(shape((rows, width), F32), shape((rows, bnd), BF16), token),
+        in_specs=[
+            VMEM,
+            VMEM,
+            row_block(hidden),
+            whole(width, hidden),
+            row_block(rows),
+            whole(rows, width),
+            ANY,
+        ],
+        out_specs=(row_block(width), row_block(bnd), token_at),
+        scratch_shapes=[pltpu.VMEM((bnd, per), BF16)],
+        compiler_params=params(LIMIT),
+        cost_estimate=cost(4 * 10**9, 10 * MIB),
+        name="own",
+    )(send_t, send_count, grad_pre, w_self, own_adj_t, gs, sent_one)
+
+    quarters = shape((half // 4, share, hidden), BF16)
+    a2, b2 = stage(
+        stage_two_kernel,
+        "stage_two",
+        [both(4, 0), both(4, 1), one(4, 1), one(4, 1), ANY],
+        (quarters, quarters),
+        (one(4, 0), one(4, 0)),
+        keep_mid,
+        core,
+        got_a1,
+        got_b1,
+        own_done,
+    )
+    got_a2, got_b2 = swap(a2, 2, parts), swap(b2, 4, parts)
+    pair = shape((2, share, hidden), BF16)
+    sent_z, base, *sends = stage(
+        stage_z_kernel,
+        "stage_z",
+        [both(4, 0), both(4, 0), one(4, 0), one(4, 0), one(4, 0), one(4, 0)],
+        (token, shape((2, share, hidden), F32), pair, pair, pair),
+        (token_at,) + (one(2, 0),) * 4,
+        keep_low,
+        core,
+        got_a1,
+        got_b1,
+        got_a2,
+        got_b2,
+    )
+    got_z = [swap(x, z << 3, parts) for z, x in enumerate(sends, 1)]
+
+    grad_features, final_done = pl.pallas_call(
+        functools.partial(final_kernel, caps),
+        grid=(steps,),
+        out_shape=(shape((rows, width), F32), token),
+        in_specs=[SMEM, row_block(width), whole(parts, sent_rows, LANES), row_block(bnd), ANY],
+        out_specs=(row_block(width), token_at),
+        scratch_shapes=[pltpu.VMEM((bnd, width), BF16)],
+        compiler_params=params(LIMIT),
+        cost_estimate=cost(10**9, 8 * MIB),
+        name="final",
+    )(hub_rows, own_grad, returned, place, sent_z)
+
+    total = shape((share, hidden), F32)
+    flat = pl.BlockSpec((share, hidden), lambda s: (0, 0))
+    grad_neigh, grad_self = stage(
+        stage_last_kernel,
+        "stage_last",
+        [one(2, 0)] * 4 + [ANY],
+        (total, total),
+        (flat, flat),
+        base,
+        *got_z,
+        final_done,
+    )
+    return layer_out, grad_features, grad_self, grad_neigh
 
 
 def on_device(
@@ -95,6 +572,15 @@
     return (layer_out, grad_features, grad_w_self, grad_w_neigh)
 
 
+def on_any_device(*args):
+    features, send_rows, hub_rows = args[0], args[7], args[9]
+    parts = lax.axis_size("dom")
+    share = features.shape[1] // parts
+    if parts == 32 and share % 8 == 0 and send_rows.shape[2] % 16 == 0 and hub_rows.shape[1] == 4:
+        return on_device_fast(*args)
+    return on_device(*args)
+
+
 def solution(mesh):
     in_specs = (
         P("dom", None),
@@ -110,5 +596,5 @@
     )
     out_specs = (P("dom", None), P("dom", None), P("dom", None), P("dom", None))
     return jax.shard_map(
-        on_device, mesh=mesh, in_specs=in_specs, out_specs=out_specs, check_vma=False
-    )
+        on_any_device, mesh=mesh, in_specs=in_specs, out_specs=out_specs, check_vma=False
+    )

time: 357 us -> 103 us (0.29)
  waiting for transfers between devices: 153 us -> 34 us
  matrix products: 67.1 us -> 0 us
  blocking collectives: 48.5 us -> 0 us
  Pallas kernels: 0 us -> 43.3 us
  local copies, waits for them, and re-layouts: 33.4 us -> 2.94 us
  other arithmetic: 23.5 us -> 0 us
  between operations: 14.3 us -> 0.74 us
  starting transfers between devices: 16.2 us -> 21.3 us
    unnamed x2 -> x0, waiting for transfers between devices: 132 us -> none
    dot_general x9 -> x0, matrix products: 67.1 us -> none  [the longest x1 28.1 us: on_device(): jnp.einsum('tks,tkjf->sjf', placement, back_terms, precision=lax.Precisio...]
    all_gather x1 -> x0, blocking collectives: 48.5 us -> none  [on_device(): hub_table = lax.all_gather(hub_mine, 'dom', axis=0, tiled=True)]
    pallas_call x0 -> x9, Pallas kernels: none -> 43.3 us  [the longest x1 17.8 us: on_device_fast(): pl.pallas_call(functools.partial(main_kernel, caps, (order(4, 2), order(2...]
    ppermute x0 -> x8, waiting for transfers between devices: none -> 16.6 us  [swap(): return lax.ppermute(x, 'dom', [(d, d ^ mask) for d in range(parts)])]
    gather x4 -> x0, local copies, waits for them, and re-layouts: 15.2 us -> none  [the longest x1 9.18 us: on_device(): picked = table_blocks[tile_src]]
    scatter-add x2 -> x0, other arithmetic: 11.7 us -> none  [the longest x1 7.38 us: on_device(): grad_features.at[rows_out.reshape(-1)]]
    ppermute x0 -> x8, starting transfers between devices: none -> 10 us  [swap(): return lax.ppermute(x, 'dom', [(d, d ^ mask) for d in range(parts)])]
  transfers between devices with their start and end apart: 4 -> 10, of which waited for: 2 -> 5; matrix products, arithmetic and copies ran while one was open for 10% -> 0% of each run, Pallas kernels for 0% -> 21%
where the time goes in v2:
time: 103 us; the launch traced here: 102 us
  Pallas kernels  43.3 us (42%)
  waiting for transfers between devices  34 us (33%)
  starting transfers between devices  21.3 us (21%)
  local copies, waits for them, and re-layouts  2.94 us (3%)
    pallas_call x1, Pallas kernels, on_device_fast(): pl.pallas_call(functools.partial(main_kernel, caps, (order(4, 2), order(2...  17.8 us
    all_to_all x1, waiting for transfers between devices, on_device_fast(): lax.all_to_all(outgoing, 'dom', split_axis=0, concat_axis=0, tiled=True)  17.4 us
    ppermute x8, waiting for transfers between devices, swap(): return lax.ppermute(x, 'dom', [(d, d ^ mask) for d in range(parts)])  16.6 us
    ppermute x8, starting transfers between devices, swap(): return lax.ppermute(x, 'dom', [(d, d ^ mask) for d in range(parts)])  10 us
    pallas_call x1, Pallas kernels, on_device_fast(): pl.pallas_call(own_kernel, grid=(steps,), out_shape=(shape((rows, width),...  7.88 us
    pallas_call x1, Pallas kernels, on_device_fast(): pl.pallas_call(early_kernel, grid=(steps,), out_shape=(shape((rows, far),...  7.44 us
    all_to_all x1, starting transfers between devices, on_device_fast(): lax.all_to_all(outgoing, 'dom', split_axis=0, concat_axis=0, tiled=True)  7.3 us
    pallas_call x1, Pallas kernels, on_device_fast(): pl.pallas_call(functools.partial(final_kernel, caps), grid=(steps,), out_...  5.6 us
  transfers between devices with their start and end apart: 10, of which 5 were waited for; matrix products, arithmetic and copies ran while one was open for 0% of the time, Pallas kernels for 21%

profile of v2, /device:TPU:0, one launch (start us, length us, event | category | flops | bytes accessed | tf_op | source)
XLA Modules:
  0.0 102.3 jit_solution(7850779343629829467)
XLA Ops:
  0.6 3.5 %pack.1 = bf16[32,120,128]{2,1,0:T(8,128)(2,1)} custom-call(s32[16,32]{1,0:T(8,128)} %bitcast.3, s32[1,32]{1,0:T(1,128)} %count_ref.5, s32[1,4]{1,0:T(1,128)} %hub_ref.3, bf16[1024,768]{1,0:T(8,128)(2,1)} %refs_4_.1), custom_call_target="tpu_custom_call" | custom-call | flops 805306368 | bytes 4194304 | tf_op jit(solution)/shard_map/pack/pallas_call | solution.py:300
  4.1 7.3 %all-to-all-start = ((bf16[32,120,128]{2,1,0:T(8,128)(2,1)}), bf16[32,120,128]{2,1,0:T(8,128)(2,1)S(1)}, u32[]{:S(2)}, u32[]{:S(2)}) async-start(bf16[32,120,128]{2,1,0:T(8,128)(2,1)} %pack.1), calls=%async_computation | async-start | bytes 1966080 | tf_op jit(solution)/shard_map/all_to_all | solution.py:310
  11.4 7.4 %early.1 = (bf16[1024,640]{1,0:T(8,128)(2,1)}, bf16[1024,1024]{1,0:T(8,128)(2,1)}, f32[1024,768]{1,0:T(8,128)}, f32[1024,128]{1,0:T(8,128)}) custom-call(s32[8,8]{1,0:T(8,128)} %src_ref.1, s32[8]{0:T(128)} %count_ref.4, bf16[8,8,128,128]{3,2,1,0:T(8,128)(2,1)} %tiles_ref.1, bf16[1024,768]{1,0:T(8,128)(2,1)} %refs_4_.1), custom_call_target="tpu_custom_call" | custom-call | flops 6000000000 | bytes 16777216 | tf_op jit(solution)/shard_map/early/pallas_call | solution.py:317
  18.9 17.4 %all-to-all-done.refs_0_ = bf16[32,120,128]{2,1,0:T(8,128)(2,1)S(1)} async-done(((bf16[32,120,128]{2,1,0:T(8,128)(2,1)}), bf16[32,120,128]{2,1,0:T(8,128)(2,1)S(1)}, u32[]{:S(2)}, u32[]{:S(2)}) %all-to-all-start) | async-done | bytes 983072 | tf_op jit(solution)/shard_map/all_to_all | solution.py:310
  36.3 0.0 copy-start.7
  36.3 1.0 copy-done.7
  37.2 17.8 %middle.1 = (bf16[1024,1024]{1,0:T(8,128)(2,1)}, bf16[1024,1024]{1,0:T(8,128)(2,1)}, bf16[1024,768]{1,0:T(8,128)(2,1)}, f32[2,4,24,1024]{3,2,1,0:T(8,128)}, f32[...) custom-call(bf16[32,120,128]{2,1,0:T(8,128)(2,1)} %copy-done.7, ...), custom_call_target="tpu_custom_call" | custom-call | flops 10000000000 | bytes 25165824 | tf_op jit(solution)/shard_map/middle/pallas_call | solution.py:355
  55.0 0.0 copy-start
  55.0 0.1 collective-permute-start
  55.1 4.0 %all-to-all-start.1 = ((bf16[32,120,128]{2,1,0:T(8,128)(2,1)}), bf16[32,120,128]{2,1,0:T(8,128)(2,1)}, u32[]{:S(2)}, u32[]{:S(2)}) async-start(bf16[32,120,128]{2,1,0:T(8,128)(2,1)} %get-tuple-element.44), calls=%async_computation.1 | async-start | bytes 1966080 | tf_op jit(solution)/shard_map/all_to_all | solution.py:377
  59.1 0.0 collective-permute-done.core_ref
  59.1 0.0 copy-done
  59.1 0.1 stage_one.1
  59.3 0.0 copy-start.6
  59.3 1.6 %collective-permute-start.1 = (bf16[8,24,1024]{2,1,0:T(8,128)(2,1)S(1)}, bf16[8,24,1024]{2,1,0:T(8,128)(2,1)S(1)}, u32[]{:S(2)}, u32[]{:S(2)}) collective-permute-start(bf16[8,24,1024]{2,1,0:T(8,128)(2,1)S(1)} %get-tuple-element.47), channel_id=1, source_target_pairs={{0,4},{1,5},{2,6},{3,7},{4,0},{5,1},{6,2},{7,3},{8,12},{9,13},{10,... | collective-permute-start | bytes 1179656 | tf_op jit(solution)/shard_map/ppermute | solution.py:266
  60.9 1.5 %collective-permute-start.2 = (bf16[8,24,1024]{2,1,0:T(8,128)(2,1)S(1)}, bf16[8,24,1024]{2,1,0:T(8,128)(2,1)S(1)}, u32[]{:S(2)}, u32[]{:S(2)}) collective-permute-start(bf16[8,24,1024]{2,1,0:T(8,128)(2,1)S(1)} %get-tuple-element.48), channel_id=1, source_target_pairs={{0,2},{1,3},{2,0},{3,1},{4,6},{5,7},{6,4},{7,5},{8,10},{9,11},{10,... | collective-permute-start | bytes 1179656 | tf_op jit(solution)/shard_map/ppermute | solution.py:266
  62.3 0.0 copy-done.6
  62.3 0.0 copy-start.2
  62.3 7.9 %own.1 = (f32[1024,768]{1,0:T(8,128)}, bf16[1024,512]{1,0:T(8,128)(2,1)}, f32[8,128]{1,0:T(8,128)}) custom-call(s32[16,32]{1,0:T(8,128)} %bitcast.4, s32[1,32]{1,0:T(1,128)} %count_ref.5, bf16[1024,1024]{1,0:T(8,128)(2,1)} %get-tuple-element.37.gp_ref, bf16[768,1024]{1,0:T(8,128)(2,1)} %w_ref.1, bf16[1024,1024]{1,0:T(8,128)(2,1)} %get-tuple-element.38.own_t_ref, ...), custom_call_target="tpu_custom_call" | custom-call | flops 4000000000 | bytes 10485760 | tf_op jit(solution)/shard_map/own/pallas_call | solution.py:407
  70.2 0.0 copy-start.1
  70.2 9.1 %collective-permute-done.1.a1_ref = bf16[8,24,1024]{2,1,0:T(8,128)(2,1)S(1)} collective-permute-done((bf16[8,24,1024]{2,1,0:T(8,128)(2,1)S(1)}, bf16[8,24,1024]{2,1,0:T(8,128)(2,1)S(1)}, u32[]{:S(2)}, u32[]{:S(2)}) %collective-permute-start.1) | collective-permute-done | bytes 393248 | tf_op jit(solution)/shard_map/ppermute | solution.py:266
  79.3 0.0 collective-permute-done.2.b1_ref
  79.3 0.0 copy-done.2
  79.3 0.0 copy-start.5
  79.3 0.7 copy-done.5
  80.0 0.1 stage_two.1
  80.1 1.9 %collective-permute-start.3 = (bf16[4,24,1024]{2,1,0:T(8,128)(2,1)S(1)}, bf16[4,24,1024]{2,1,0:T(8,128)(2,1)S(1)}, u32[]{:S(2)}, u32[]{:S(2)}) collective-permute-start(bf16[4,24,1024]{2,1,0:T(8,128)(2,1)S(1)} %get-tuple-element.51), channel_id=1, source_target_pairs={{0,2},{1,3},{2,0},{3,1},{4,6},{5,7},{6,4},{7,5},{8,10},{9,11},{10,... | collective-permute-start | bytes 589832 | tf_op jit(solution)/shard_map/ppermute | solution.py:266
  82.0 0.3 collective-permute-start.4
  82.3 4.8 %collective-permute-done.3.a2_ref = bf16[4,24,1024]{2,1,0:T(8,128)(2,1)S(1)} collective-permute-done((bf16[4,24,1024]{2,1,0:T(8,128)(2,1)S(1)}, bf16[4,24,1024]{2,1,0:T(8,128)(2,1)S(1)}, u32[]{:S(2)}, u32[]{:S(2)}) %collective-permute-start.3) | collective-permute-done | bytes 196640 | tf_op jit(solution)/shard_map/ppermute | solution.py:266
  87.1 1.3 %collective-permute-done.4.b2_ref = bf16[4,24,1024]{2,1,0:T(8,128)(2,1)S(1)} collective-permute-done((bf16[4,24,1024]{2,1,0:T(8,128)(2,1)S(1)}, bf16[4,24,1024]{2,1,0:T(8,128)(2,1)S(1)}, u32[]{:S(2)}, u32[]{:S(2)}) %collective-permute-start.4) | collective-permute-done | bytes 196640 | tf_op jit(solution)/shard_map/ppermute | solution.py:266
  88.4 0.0 copy-done.1
  88.4 0.2 stage_z.1
  88.6 0.0 copy-start.3
  88.6 0.6 copy-done.3
  89.2 1.5 %collective-permute-start.5 = (bf16[2,24,1024]{2,1,0:T(8,128)(2,1)S(1)}, bf16[2,24,1024]{2,1,0:T(8,128)(2,1)S(1)}, u32[]{:S(2)}, u32[]{:S(2)}) collective-permute-start(bf16[2,24,1024]{2,1,0:T(8,128)(2,1)S(1)} %get-tuple-element.56), channel_id=1, source_target_pairs={{0,8},{1,9},{2,10},{3,11},{4,12},{5,13},{6,14},{7,15},{8,0},{9,1},... | collective-permute-start | bytes 294920 | tf_op jit(solution)/shard_map/ppermute | solution.py:266
  90.7 2.9 %collective-permute-start.6 = (bf16[2,24,1024]{2,1,0:T(8,128)(2,1)S(1)}, bf16[2,24,1024]{2,1,0:T(8,128)(2,1)S(1)}, u32[]{:S(2)}, u32[]{:S(2)}) collective-permute-start(bf16[2,24,1024]{2,1,0:T(8,128)(2,1)S(1)} %get-tuple-element.57), channel_id=1, source_target_pairs={{0,16},{1,17},{2,18},{3,19},{4,20},{5,21},{6,22},{7,23},{8,24},{9,... | collective-permute-start | bytes 294920 | tf_op jit(solution)/shard_map/ppermute | solution.py:266
  93.6 0.3 collective-permute-start.7
  93.9 0.0 all-to-all-done.1.got_ref
  93.9 5.6 %final.1 = (f32[1024,768]{1,0:T(8,128)}, f32[8,128]{1,0:T(8,128)}) custom-call(s32[1,4]{1,0:T(1,128)} %hub_ref.3, f32[1024,768]{1,0:T(8,128)} %get-tuple-element.43.own_ref, bf16[32,120,128]{2,1,0:T(8,128)(2,1)} %all-to-all-done.1.got_ref, bf16[1024,512]{1,0:T(8,128)(2,1)} %get-tuple-element.45.place_ref, f32[8,128]{1,0:T(8,128)} %copy-done.3), custom_call_target="tpu_custom_call" | custom-call | flops 1000000000 | bytes 8388608 | tf_op jit(solution)/shard_map/final/pallas_call | solution.py:457
  99.5 0.0 collective-permute-done.5.z1_ref
  99.5 1.4 %collective-permute-done.6.z2_ref = bf16[2,24,1024]{2,1,0:T(8,128)(2,1)S(1)} collective-permute-done((bf16[2,24,1024]{2,1,0:T(8,128)(2,1)S(1)}, bf16[2,24,1024]{2,1,0:T(8,128)(2,1)S(1)}, u32[]{:S(2)}, u32[]{:S(2)}) %collective-permute-start.6) | collective-permute-done | bytes 98336 | tf_op jit(solution)/shard_map/ppermute | solution.py:266
  100.9 0.0 collective-permute-done.7.z3_ref
  100.9 0.0 copy-start.4
  100.9 0.7 copy-done.4
  101.6 0.7 stage_last.1
Async XLA Ops:
  4.1 32.1 %all-to-all-start = ((bf16[32,120,128]{2,1,0:T(8,128)(2,1)}), bf16[32,120,128]{2,1,0:T(8,128)(2,1)S(1)}, u32[]{:S(2)}, u32[]{:S(2)}) async-start(bf16[32,120,128]{2,1,0:T(8,128)(2,1)} %pack.1), calls=%async_computation | async-start | bytes 1966080 | tf_op jit(solution)/shard_map/all_to_all | solution.py:310
  36.3 1.0 copy-start.7
  55.0 4.1 %copy-start = (f32[2,8,24,1024]{3,2,1,0:T(8,128)S(1)}, f32[2,8,24,1024]{3,2,1,0:T(8,128)}, u32[]{:S(2)}) copy-start(f32[2,8,24,1024]{3,2,1,0:T(8,128)} %get-tuple-element.40.keep_ref) | copy-start | bytes 4718596
  55.0 4.1 %collective-permute-start = (bf16[2,16,24,1024]{3,2,1,0:T(8,128)(2,1)}, bf16[2,16,24,1024]{3,2,1,0:T(8,128)(2,1)S(1)}, u32[]{:S(2)}, u32[]{:S(2)}) collective-permute-start(bf16[2,16,24,1024]{3,2,1,0:T(8,128)(2,1)} %get-tuple-element.41), channel_id=1, source_target_pairs={{0,1},{1,0},{2,3},{3,2},{4,5},{5,4},{6,7},{7,6},{8,9},{9,8},{10,11... | collective-permute-start | bytes 4718600 | tf_op jit(solution)/shard_map/ppermute | solution.py:266
  55.1 38.9 %all-to-all-start.1 = ((bf16[32,120,128]{2,1,0:T(8,128)(2,1)}), bf16[32,120,128]{2,1,0:T(8,128)(2,1)}, u32[]{:S(2)}, u32[]{:S(2)}) async-start(bf16[32,120,128]{2,1,0:T(8,128)(2,1)} %get-tuple-element.44), calls=%async_computation.1 | async-start | bytes 1966080 | tf_op jit(solution)/shard_map/all_to_all | solution.py:377
  59.3 3.1 %copy-start.6 = (f32[8,128]{1,0:T(8,128)}, f32[8,128]{1,0:T(8,128)S(1)}, u32[]{:S(2)}) copy-start(f32[8,128]{1,0:T(8,128)S(1)} %get-tuple-element.42._) | copy-start | bytes 12292
  59.3 20.0 %collective-permute-start.1 = (bf16[8,24,1024]{2,1,0:T(8,128)(2,1)S(1)}, bf16[8,24,1024]{2,1,0:T(8,128)(2,1)S(1)}, u32[]{:S(2)}, u32[]{:S(2)}) collective-permute-start(bf16[8,24,1024]{2,1,0:T(8,128)(2,1)S(1)} %get-tuple-element.47), channel_id=1, source_target_pairs={{0,4},{1,5},{2,6},{3,7},{4,0},{5,1},{6,2},{7,3},{8,12},{9,13},{10,... | collective-permute-start | bytes 1179656 | tf_op jit(solution)/shard_map/ppermute | solution.py:266
  60.9 18.4 %collective-permute-start.2 = (bf16[8,24,1024]{2,1,0:T(8,128)(2,1)S(1)}, bf16[8,24,1024]{2,1,0:T(8,128)(2,1)S(1)}, u32[]{:S(2)}, u32[]{:S(2)}) collective-permute-start(bf16[8,24,1024]{2,1,0:T(8,128)(2,1)S(1)} %get-tuple-element.48), channel_id=1, source_target_pairs={{0,2},{1,3},{2,0},{3,1},{4,6},{5,7},{6,4},{7,5},{8,10},{9,11},{10,... | collective-permute-start | bytes 1179656 | tf_op jit(solution)/shard_map/ppermute | solution.py:266
  62.3 17.0 %copy-start.2 = (f32[2,4,24,1024]{3,2,1,0:T(8,128)S(1)}, f32[2,4,24,1024]{3,2,1,0:T(8,128)}, u32[]{:S(2)}) copy-start(f32[2,4,24,1024]{3,2,1,0:T(8,128)} %get-tuple-element.49.keep_ref) | copy-start | bytes 2359300
  70.2 18.2 %copy-start.1 = (f32[2,4,24,1024]{3,2,1,0:T(8,128)S(1)}, f32[2,4,24,1024]{3,2,1,0:T(8,128)}, u32[]{:S(2)}) copy-start(f32[2,4,24,1024]{3,2,1,0:T(8,128)} %get-tuple-element.46.keep_ref) | copy-start | bytes 2359300
  79.3 0.7 copy-start.5
  80.1 7.0 %collective-permute-start.3 = (bf16[4,24,1024]{2,1,0:T(8,128)(2,1)S(1)}, bf16[4,24,1024]{2,1,0:T(8,128)(2,1)S(1)}, u32[]{:S(2)}, u32[]{:S(2)}) collective-permute-start(bf16[4,24,1024]{2,1,0:T(8,128)(2,1)S(1)} %get-tuple-element.51), channel_id=1, source_target_pairs={{0,2},{1,3},{2,0},{3,1},{4,6},{5,7},{6,4},{7,5},{8,10},{9,11},{10,... | collective-permute-start | bytes 589832 | tf_op jit(solution)/shard_map/ppermute | solution.py:266
  82.0 6.4 %collective-permute-start.4 = (bf16[4,24,1024]{2,1,0:T(8,128)(2,1)S(1)}, bf16[4,24,1024]{2,1,0:T(8,128)(2,1)S(1)}, u32[]{:S(2)}, u32[]{:S(2)}) collective-permute-start(bf16[4,24,1024]{2,1,0:T(8,128)(2,1)S(1)} %get-tuple-element.52), channel_id=1, source_target_pairs={{0,4},{1,5},{2,6},{3,7},{4,0},{5,1},{6,2},{7,3},{8,12},{9,13},{10,... | collective-permute-start | bytes 589832 | tf_op jit(solution)/shard_map/ppermute | solution.py:266
  88.6 0.6 copy-start.3
  89.2 10.4 %collective-permute-start.5 = (bf16[2,24,1024]{2,1,0:T(8,128)(2,1)S(1)}, bf16[2,24,1024]{2,1,0:T(8,128)(2,1)S(1)}, u32[]{:S(2)}, u32[]{:S(2)}) collective-permute-start(bf16[2,24,1024]{2,1,0:T(8,128)(2,1)S(1)} %get-tuple-element.56), channel_id=1, source_target_pairs={{0,8},{1,9},{2,10},{3,11},{4,12},{5,13},{6,14},{7,15},{8,0},{9,1},... | collective-permute-start | bytes 294920 | tf_op jit(solution)/shard_map/ppermute | solution.py:266
  90.7 10.2 %collective-permute-start.6 = (bf16[2,24,1024]{2,1,0:T(8,128)(2,1)S(1)}, bf16[2,24,1024]{2,1,0:T(8,128)(2,1)S(1)}, u32[]{:S(2)}, u32[]{:S(2)}) collective-permute-start(bf16[2,24,1024]{2,1,0:T(8,128)(2,1)S(1)} %get-tuple-element.57), channel_id=1, source_target_pairs={{0,16},{1,17},{2,18},{3,19},{4,20},{5,21},{6,22},{7,23},{8,24},{9,... | collective-permute-start | bytes 294920 | tf_op jit(solution)/shard_map/ppermute | solution.py:266
  93.6 7.3 %collective-permute-start.7 = (bf16[2,24,1024]{2,1,0:T(8,128)(2,1)S(1)}, bf16[2,24,1024]{2,1,0:T(8,128)(2,1)S(1)}, u32[]{:S(2)}, u32[]{:S(2)}) collective-permute-start(bf16[2,24,1024]{2,1,0:T(8,128)(2,1)S(1)} %get-tuple-element.58), channel_id=1, source_target_pairs={{0,24},{1,25},{2,26},{3,27},{4,28},{5,29},{6,30},{7,31},{8,16},{9,... | collective-permute-start | bytes 294920 | tf_op jit(solution)/shard_map/ppermute | solution.py:266
  100.9 0.7 copy-start.4

commit v3 on v2

--- a/solution.py
+++ b/solution.py
@@ -218,7 +218,7 @@
             ref[chain] = total[z + 1].astype(BF16)
 
 
-def stage_last_kernel(base_ref, z1_ref, z2_ref, z3_ref, _, neigh_ref, self_ref):
+def stage_last_kernel(base_ref, z1_ref, z2_ref, z3_ref, neigh_ref, self_ref):
     for chain, ref in ((0, neigh_ref), (1, self_ref)):
         total = base_ref[chain] + z1_ref[chain].astype(F32)
         ref[...] = total + z2_ref[chain].astype(F32) + z3_ref[chain].astype(F32)
@@ -237,7 +237,7 @@
     place_ref[...] = hits[...].T
 
 
-def final_kernel(caps, hub_ref, own_ref, got_ref, place_ref, _, out_ref, token_ref, rows):
+def final_kernel(caps, hub_ref, own_ref, got_ref, place_ref, out_ref, token_ref, rows):
     token_ref[...] = jnp.zeros_like(token_ref)
     step = pl.program_id(0)
     parts = got_ref.shape[0]
@@ -419,7 +419,7 @@
         ],
         out_specs=(row_block(width), row_block(bnd), token_at),
         scratch_shapes=[pltpu.VMEM((bnd, per), BF16)],
-        compiler_params=params(LIMIT),
+        compiler_params=params(24),
         cost_estimate=cost(4 * 10**9, 10 * MIB),
         name="own",
     )(send_t, send_count, grad_pre, w_self, own_adj_t, gs, sent_one)
@@ -452,31 +452,30 @@
         got_a2,
         got_b2,
     )
-    got_z = [swap(x, z << 3, parts) for z, x in enumerate(sends, 1)]
+    got_z = [swap(sends[z - 1], z << 3, parts) for z in (2, 3, 1)]
 
     grad_features, final_done = pl.pallas_call(
         functools.partial(final_kernel, caps),
         grid=(steps,),
         out_shape=(shape((rows, width), F32), token),
-        in_specs=[SMEM, row_block(width), whole(parts, sent_rows, LANES), row_block(bnd), ANY],
+        in_specs=[SMEM, row_block(width), whole(parts, sent_rows, LANES), row_block(bnd)],
         out_specs=(row_block(width), token_at),
         scratch_shapes=[pltpu.VMEM((bnd, width), BF16)],
         compiler_params=params(LIMIT),
         cost_estimate=cost(10**9, 8 * MIB),
         name="final",
-    )(hub_rows, own_grad, returned, place, sent_z)
+    )(hub_rows, own_grad, returned, place)
 
     total = shape((share, hidden), F32)
     flat = pl.BlockSpec((share, hidden), lambda s: (0, 0))
     grad_neigh, grad_self = stage(
         stage_last_kernel,
         "stage_last",
-        [one(2, 0)] * 4 + [ANY],
+        [one(2, 0)] * 4,
         (total, total),
         (flat, flat),
         base,
         *got_z,
-        final_done,
     )
     return layer_out, grad_features, grad_self, grad_neigh
 

time: 103 us -> 100 us (0.971)
  Pallas kernels: 43.3 us -> 39.9 us
  local copies, waits for them, and re-layouts: 2.94 us -> 4.2 us
    pallas_call x1, Pallas kernels: 7.88 us -> 3.98 us  [on_device_fast(): pl.pallas_call(own_kernel, grid=(steps,), out_shape=(shape((rows, width),...]
    unnamed x16 -> x24, local copies, waits for them, and re-layouts: 2.94 us -> 4.2 us
  transfers between devices with their start and end apart: 10 -> 10, of which waited for: 5 -> 6; matrix products, arithmetic and copies ran while one was open for 0% -> 0% of each run, Pallas kernels for 21% -> 18%
where the time goes in v3:
time: 100 us; the launch traced here: 99.7 us
  Pallas kernels  39.9 us (40%)
  waiting for transfers between devices  33.8 us (34%)
  starting transfers between devices  21 us (21%)
  local copies, waits for them, and re-layouts  4.2 us (4%)
    pallas_call x1, Pallas kernels, on_device_fast(): pl.pallas_call(functools.partial(main_kernel, caps, (order(4, 2), order(2...  17.8 us
    all_to_all x1, waiting for transfers between devices, on_device_fast(): lax.all_to_all(outgoing, 'dom', split_axis=0, concat_axis=0, tiled=True)  17.4 us
    ppermute x8, waiting for transfers between devices, swap(): return lax.ppermute(x, 'dom', [(d, d ^ mask) for d in range(parts)])  16.4 us
    ppermute x8, starting transfers between devices, swap(): return lax.ppermute(x, 'dom', [(d, d ^ mask) for d in range(parts)])  9.69 us
    pallas_call x1, Pallas kernels, on_device_fast(): pl.pallas_call(early_kernel, grid=(steps,), out_shape=(shape((rows, far),...  7.44 us
    all_to_all x1, starting transfers between devices, on_device_fast(): lax.all_to_all(outgoing, 'dom', split_axis=0, concat_axis=0, tiled=True)  7.3 us
    pallas_call x1, Pallas kernels, on_device_fast(): pl.pallas_call(functools.partial(final_kernel, caps), grid=(steps,), out_...  5.6 us
    unnamed x24, local copies, waits for them, and re-layouts  4.2 us
  transfers between devices with their start and end apart: 10, of which 6 were waited for; matrix products, arithmetic and copies ran while one was open for 0% of the time, Pallas kernels for 18%

profile of v3, /device:TPU:0, one launch (start us, length us, event | category | flops | bytes accessed | tf_op | source)
XLA Modules:
  0.0 99.7 jit_solution(1869315811392691481)
XLA Ops:
  0.6 3.5 %pack.1 = bf16[32,120,128]{2,1,0:T(8,128)(2,1)} custom-call(s32[16,32]{1,0:T(8,128)} %bitcast.3, s32[1,32]{1,0:T(1,128)} %count_ref.5, s32[1,4]{1,0:T(1,128)} %hub_ref.3, bf16[1024,768]{1,0:T(8,128)(2,1)} %refs_4_.1), custom_call_target="tpu_custom_call" | custom-call | flops 805306368 | bytes 4194304 | tf_op jit(solution)/shard_map/pack/pallas_call | solution.py:300
  4.1 7.3 %all-to-all-start = ((bf16[32,120,128]{2,1,0:T(8,128)(2,1)}), bf16[32,120,128]{2,1,0:T(8,128)(2,1)S(1)}, u32[]{:S(2)}, u32[]{:S(2)}) async-start(bf16[32,120,128]{2,1,0:T(8,128)(2,1)} %pack.1), calls=%async_computation | async-start | bytes 1966080 | tf_op jit(solution)/shard_map/all_to_all | solution.py:310
  11.4 7.4 %early.1 = (bf16[1024,640]{1,0:T(8,128)(2,1)}, bf16[1024,1024]{1,0:T(8,128)(2,1)}, f32[1024,768]{1,0:T(8,128)}, f32[1024,128]{1,0:T(8,128)}) custom-call(s32[8,8]{1,0:T(8,128)} %src_ref.1, s32[8]{0:T(128)} %count_ref.4, bf16[8,8,128,128]{3,2,1,0:T(8,128)(2,1)} %tiles_ref.1, bf16[1024,768]{1,0:T(8,128)(2,1)} %refs_4_.1), custom_call_target="tpu_custom_call" | custom-call | flops 6000000000 | bytes 16777216 | tf_op jit(solution)/shard_map/early/pallas_call | solution.py:317
  18.9 17.4 %all-to-all-done.refs_0_ = bf16[32,120,128]{2,1,0:T(8,128)(2,1)S(1)} async-done(((bf16[32,120,128]{2,1,0:T(8,128)(2,1)}), bf16[32,120,128]{2,1,0:T(8,128)(2,1)S(1)}, u32[]{:S(2)}, u32[]{:S(2)}) %all-to-all-start) | async-done | bytes 983072 | tf_op jit(solution)/shard_map/all_to_all | solution.py:310
  36.3 1.0 copy-done.11
  37.2 17.8 %middle.1 = (bf16[1024,1024]{1,0:T(8,128)(2,1)}, bf16[1024,1024]{1,0:T(8,128)(2,1)}, bf16[1024,768]{1,0:T(8,128)(2,1)}, f32[2,4,24,1024]{3,2,1,0:T(8,128)}, f32[...) custom-call(bf16[32,120,128]{2,1,0:T(8,128)(2,1)} %copy-done.11, ...), custom_call_target="tpu_custom_call" | custom-call | flops 10000000000 | bytes 25165824 | tf_op jit(solution)/shard_map/middle/pallas_call | solution.py:355
  55.0 0.0 copy-start.1
  55.0 0.1 collective-permute-start
  55.1 0.0 copy-start.6
  55.1 0.0 copy-start.7
  55.1 4.0 %all-to-all-start.1 = ((bf16[32,120,128]{2,1,0:T(8,128)(2,1)}), bf16[32,120,128]{2,1,0:T(8,128)(2,1)}, u32[]{:S(2)}, u32[]{:S(2)}) async-start(bf16[32,120,128]{2,1,0:T(8,128)(2,1)} %get-tuple-element.42), calls=%async_computation.1 | async-start | bytes 1966080 | tf_op jit(solution)/shard_map/all_to_all | solution.py:377
  59.1 0.0 copy-start.5
  59.1 0.0 copy-start.10
  59.1 0.0 collective-permute-done.core_ref
  59.1 0.0 copy-done.1
  59.2 0.2 stage_one.1
  59.3 1.6 %collective-permute-start.1 = (bf16[8,24,1024]{2,1,0:T(8,128)(2,1)S(1)}, bf16[8,24,1024]{2,1,0:T(8,128)(2,1)S(1)}, u32[]{:S(2)}, u32[]{:S(2)}) collective-permute-start(bf16[8,24,1024]{2,1,0:T(8,128)(2,1)S(1)} %get-tuple-element.46), channel_id=1, source_target_pairs={{0,4},{1,5},{2,6},{3,7},{4,0},{5,1},{6,2},{7,3},{8,12},{9,13},{10,... | collective-permute-start | bytes 1179656 | tf_op jit(solution)/shard_map/ppermute | solution.py:266
  60.9 1.5 %collective-permute-start.2 = (bf16[8,24,1024]{2,1,0:T(8,128)(2,1)S(1)}, bf16[8,24,1024]{2,1,0:T(8,128)(2,1)S(1)}, u32[]{:S(2)}, u32[]{:S(2)}) collective-permute-start(bf16[8,24,1024]{2,1,0:T(8,128)(2,1)S(1)} %get-tuple-element.47), channel_id=1, source_target_pairs={{0,2},{1,3},{2,0},{3,1},{4,6},{5,7},{6,4},{7,5},{8,10},{9,11},{10,... | collective-permute-start | bytes 1179656 | tf_op jit(solution)/shard_map/ppermute | solution.py:266
  62.4 0.0 copy-done.6
  62.4 0.0 copy-done.7
  62.4 0.0 copy-done.5
  62.4 0.0 copy-done.10
  62.4 0.0 copy-start.8
  62.4 1.6 %copy-done.8 = bf16[1024,1024]{1,0:T(8,128)(2,1)S(1)} copy-done((bf16[1024,1024]{1,0:T(8,128)(2,1)S(1)}, bf16[1024,1024]{1,0:T(8,128)(2,1)}, u32[]{:S(2)}) %copy-start.8) | copy-done | bytes 2097176
  64.0 1.6 %copy-done.9 = bf16[1024,1024]{1,0:T(8,128)(2,1)S(1)} copy-done((bf16[1024,1024]{1,0:T(8,128)(2,1)S(1)}, bf16[1024,1024]{1,0:T(8,128)(2,1)}, u32[]{:S(2)}) %copy-start.9) | copy-done | bytes 2097176
  65.6 4.0 %own.1 = (f32[1024,768]{1,0:T(8,128)S(1)}, bf16[1024,512]{1,0:T(8,128)(2,1)S(1)}, f32[8,128]{1,0:T(8,128)S(1)}) custom-call(s32[16,32]{1,0:T(8,128)S(1)} %bitcast.4, s32[1,32]{1,0:T(1,128)S(1)} %copy-done.7, bf16[1024,1024]{1,0:T(8,128)(2,1)S(1)} %copy-done.9, bf16[768,1024]{1,0:T(8,128)(2,1)S(1)} %copy-done.5, bf16[1024,1024]{1,0:T(8,128)(2,1)S(1)} %copy-done.8, ...), custom_call_target="tpu_custom_call" | custom-call | flops 4000000000 | bytes 10485760 | tf_op jit(solution)/shard_map/own/pallas_call | solution.py:407
  69.6 0.0 copy-start
  69.6 0.0 copy-start.2
  69.6 0.0 copy-start.3
  69.6 9.7 %collective-permute-done.1.a1_ref = bf16[8,24,1024]{2,1,0:T(8,128)(2,1)S(1)} collective-permute-done((bf16[8,24,1024]{2,1,0:T(8,128)(2,1)S(1)}, bf16[8,24,1024]{2,1,0:T(8,128)(2,1)S(1)}, u32[]{:S(2)}, u32[]{:S(2)}) %collective-permute-start.1) | collective-permute-done | bytes 393248 | tf_op jit(solution)/shard_map/ppermute | solution.py:266
  79.3 0.0 collective-permute-done.2.b1_ref
  79.3 0.0 copy-done.4
  79.3 0.1 stage_two.1
  79.5 1.9 %collective-permute-start.3 = (bf16[4,24,1024]{2,1,0:T(8,128)(2,1)S(1)}, bf16[4,24,1024]{2,1,0:T(8,128)(2,1)S(1)}, u32[]{:S(2)}, u32[]{:S(2)}) collective-permute-start(bf16[4,24,1024]{2,1,0:T(8,128)(2,1)S(1)} %get-tuple-element.50), channel_id=1, source_target_pairs={{0,2},{1,3},{2,0},{3,1},{4,6},{5,7},{6,4},{7,5},{8,10},{9,11},{10,... | collective-permute-start | bytes 589832 | tf_op jit(solution)/shard_map/ppermute | solution.py:266
  81.3 0.3 collective-permute-start.4
  81.6 5.0 %collective-permute-done.3.a2_ref = bf16[4,24,1024]{2,1,0:T(8,128)(2,1)S(1)} collective-permute-done((bf16[4,24,1024]{2,1,0:T(8,128)(2,1)S(1)}, bf16[4,24,1024]{2,1,0:T(8,128)(2,1)S(1)}, u32[]{:S(2)}, u32[]{:S(2)}) %collective-permute-start.3) | collective-permute-done | bytes 196640 | tf_op jit(solution)/shard_map/ppermute | solution.py:266
  86.6 1.1 %collective-permute-done.4.b2_ref = bf16[4,24,1024]{2,1,0:T(8,128)(2,1)S(1)} collective-permute-done((bf16[4,24,1024]{2,1,0:T(8,128)(2,1)S(1)}, bf16[4,24,1024]{2,1,0:T(8,128)(2,1)S(1)}, u32[]{:S(2)}, u32[]{:S(2)}) %collective-permute-start.4) | collective-permute-done | bytes 196640 | tf_op jit(solution)/shard_map/ppermute | solution.py:266
  87.8 0.0 copy-done.3
  87.8 0.7 stage_z.1
  88.4 3.3 %collective-permute-start.5 = (bf16[2,24,1024]{2,1,0:T(8,128)(2,1)S(1)}, bf16[2,24,1024]{2,1,0:T(8,128)(2,1)S(1)}, u32[]{:S(2)}, u32[]{:S(2)}) collective-permute-start(bf16[2,24,1024]{2,1,0:T(8,128)(2,1)S(1)} %get-tuple-element.53), channel_id=1, source_target_pairs={{0,16},{1,17},{2,18},{3,19},{4,20},{5,21},{6,22},{7,23},{8,24},{9,... | collective-permute-start | bytes 294920 | tf_op jit(solution)/shard_map/ppermute | solution.py:266
  91.7 0.6 collective-permute-start.6
  92.4 0.5 collective-permute-start.7
  92.9 0.0 all-to-all-done.1.got_ref
  92.9 5.6 %final.1 = (f32[1024,768]{1,0:T(8,128)}, f32[8,128]{1,0:T(8,128)}) custom-call(s32[1,4]{1,0:T(1,128)} %hub_ref.3, f32[1024,768]{1,0:T(8,128)} %copy-done, bf16[32,120,128]{2,1,0:T(8,128)(2,1)} %all-to-all-done.1.got_ref, bf16[1024,512]{1,0:T(8,128)(2,1)} %copy-done.2), custom_call_target="tpu_custom_call" | custom-call | flops 1000000000 | bytes 8388608 | tf_op jit(solution)/shard_map/final/pallas_call | solution.py:457
  98.5 0.2 collective-permute-done.5.z1_ref
  98.6 0.0 collective-permute-done.6.z2_ref
  98.6 0.3 collective-permute-done.7.z3_ref
  99.0 0.7 stage_last.1
  (5 shorter events, 0.0 us)
Async XLA Ops:
  4.1 32.1 %all-to-all-start = ((bf16[32,120,128]{2,1,0:T(8,128)(2,1)}), bf16[32,120,128]{2,1,0:T(8,128)(2,1)S(1)}, u32[]{:S(2)}, u32[]{:S(2)}) async-start(bf16[32,120,128]{2,1,0:T(8,128)(2,1)} %pack.1), calls=%async_computation | async-start | bytes 1966080 | tf_op jit(solution)/shard_map/all_to_all | solution.py:310
  36.3 1.0 copy-start.11
  55.0 4.1 %copy-start.1 = (f32[2,8,24,1024]{3,2,1,0:T(8,128)S(1)}, f32[2,8,24,1024]{3,2,1,0:T(8,128)}, u32[]{:S(2)}) copy-start(f32[2,8,24,1024]{3,2,1,0:T(8,128)} %get-tuple-element.38.keep_ref) | copy-start | bytes 4718596
  55.0 4.1 %collective-permute-start = (bf16[2,16,24,1024]{3,2,1,0:T(8,128)(2,1)}, bf16[2,16,24,1024]{3,2,1,0:T(8,128)(2,1)S(1)}, u32[]{:S(2)}, u32[]{:S(2)}) collective-permute-start(bf16[2,16,24,1024]{3,2,1,0:T(8,128)(2,1)} %get-tuple-element.39), channel_id=1, source_target_pairs={{0,1},{1,0},{2,3},{3,2},{4,5},{5,4},{6,7},{7,6},{8,9},{9,8},{10,11... | collective-permute-start | bytes 4718600 | tf_op jit(solution)/shard_map/ppermute | solution.py:266
  55.1 7.3 %copy-start.6 = (s32[1,32,16]{1,2,0:T(8,128)S(1)}, s32[1,32,16]{1,2,0:T(8,128)}, u32[]{:S(2)}) copy-start(s32[1,32,16]{1,2,0:T(8,128)} %param.17) | copy-start | bytes 6148
  55.1 7.3 %copy-start.7 = (s32[1,32]{1,0:T(1,128)S(1)}, s32[1,32]{1,0:T(1,128)}, u32[]{:S(2)}) copy-start(s32[1,32]{1,0:T(1,128)} %count_ref.5) | copy-start | bytes 388
  55.1 37.8 %all-to-all-start.1 = ((bf16[32,120,128]{2,1,0:T(8,128)(2,1)}), bf16[32,120,128]{2,1,0:T(8,128)(2,1)}, u32[]{:S(2)}, u32[]{:S(2)}) async-start(bf16[32,120,128]{2,1,0:T(8,128)(2,1)} %get-tuple-element.42), calls=%async_computation.1 | async-start | bytes 1966080 | tf_op jit(solution)/shard_map/all_to_all | solution.py:377
  59.1 3.3 %copy-start.5 = (bf16[768,1024]{1,0:T(8,128)(2,1)S(1)}, bf16[768,1024]{1,0:T(8,128)(2,1)}, u32[]{:S(2)}) copy-start(bf16[768,1024]{1,0:T(8,128)(2,1)} %w_ref.1) | copy-start | bytes 4718596
  59.1 3.3 %copy-start.10 = (bf16[1024,768]{1,0:T(8,128)(2,1)S(1)}, bf16[1024,768]{1,0:T(8,128)(2,1)}, u32[]{:S(2)}) copy-start(bf16[1024,768]{1,0:T(8,128)(2,1)} %get-tuple-element.37.gs_ref) | copy-start | bytes 4718596
  59.3 20.0 %collective-permute-start.1 = (bf16[8,24,1024]{2,1,0:T(8,128)(2,1)S(1)}, bf16[8,24,1024]{2,1,0:T(8,128)(2,1)S(1)}, u32[]{:S(2)}, u32[]{:S(2)}) collective-permute-start(bf16[8,24,1024]{2,1,0:T(8,128)(2,1)S(1)} %get-tuple-element.46), channel_id=1, source_target_pairs={{0,4},{1,5},{2,6},{3,7},{4,0},{5,1},{6,2},{7,3},{8,12},{9,13},{10,... | collective-permute-start | bytes 1179656 | tf_op jit(solution)/shard_map/ppermute | solution.py:266
  60.9 18.4 %collective-permute-start.2 = (bf16[8,24,1024]{2,1,0:T(8,128)(2,1)S(1)}, bf16[8,24,1024]{2,1,0:T(8,128)(2,1)S(1)}, u32[]{:S(2)}, u32[]{:S(2)}) collective-permute-start(bf16[8,24,1024]{2,1,0:T(8,128)(2,1)S(1)} %get-tuple-element.47), channel_id=1, source_target_pairs={{0,2},{1,3},{2,0},{3,1},{4,6},{5,7},{6,4},{7,5},{8,10},{9,11},{10,... | collective-permute-start | bytes 1179656 | tf_op jit(solution)/shard_map/ppermute | solution.py:266
  62.4 1.6 %copy-start.8 = (bf16[1024,1024]{1,0:T(8,128)(2,1)S(1)}, bf16[1024,1024]{1,0:T(8,128)(2,1)}, u32[]{:S(2)}) copy-start(bf16[1024,1024]{1,0:T(8,128)(2,1)} %get-tuple-element.36.own_t_ref) | copy-start | bytes 6291460
  64.0 1.6 %copy-start.9 = (bf16[1024,1024]{1,0:T(8,128)(2,1)S(1)}, bf16[1024,1024]{1,0:T(8,128)(2,1)}, u32[]{:S(2)}) copy-start(bf16[1024,1024]{1,0:T(8,128)(2,1)} %get-tuple-element.35.gp_ref) | copy-start | bytes 6291460
  65.6 13.7 %copy-start.4 = (f32[2,4,24,1024]{3,2,1,0:T(8,128)S(1)}, f32[2,4,24,1024]{3,2,1,0:T(8,128)}, u32[]{:S(2)}) copy-start(f32[2,4,24,1024]{3,2,1,0:T(8,128)} %get-tuple-element.48.keep_ref) | copy-start | bytes 2359300
  69.6 18.9 %copy-start = (f32[1024,768]{1,0:T(8,128)}, f32[1024,768]{1,0:T(8,128)S(1)}, u32[]{:S(2)}) copy-start(f32[1024,768]{1,0:T(8,128)S(1)} %get-tuple-element.41.own_ref) | copy-start | bytes 9437188
  69.6 18.9 %copy-start.2 = (bf16[1024,512]{1,0:T(8,128)(2,1)}, bf16[1024,512]{1,0:T(8,128)(2,1)S(1)}, u32[]{:S(2)}) copy-start(bf16[1024,512]{1,0:T(8,128)(2,1)S(1)} %get-tuple-element.43.place_ref) | copy-start | bytes 3145732
  69.6 18.2 %copy-start.3 = (f32[2,4,24,1024]{3,2,1,0:T(8,128)S(1)}, f32[2,4,24,1024]{3,2,1,0:T(8,128)}, u32[]{:S(2)}) copy-start(f32[2,4,24,1024]{3,2,1,0:T(8,128)} %get-tuple-element.45.keep_ref) | copy-start | bytes 2359300
  79.5 7.2 %collective-permute-start.3 = (bf16[4,24,1024]{2,1,0:T(8,128)(2,1)S(1)}, bf16[4,24,1024]{2,1,0:T(8,128)(2,1)S(1)}, u32[]{:S(2)}, u32[]{:S(2)}) collective-permute-start(bf16[4,24,1024]{2,1,0:T(8,128)(2,1)S(1)} %get-tuple-element.50), channel_id=1, source_target_pairs={{0,2},{1,3},{2,0},{3,1},{4,6},{5,7},{6,4},{7,5},{8,10},{9,11},{10,... | collective-permute-start | bytes 589832 | tf_op jit(solution)/shard_map/ppermute | solution.py:266
  81.3 6.4 %collective-permute-start.4 = (bf16[4,24,1024]{2,1,0:T(8,128)(2,1)S(1)}, bf16[4,24,1024]{2,1,0:T(8,128)(2,1)S(1)}, u32[]{:S(2)}, u32[]{:S(2)}) collective-permute-start(bf16[4,24,1024]{2,1,0:T(8,128)(2,1)S(1)} %get-tuple-element.51), channel_id=1, source_target_pairs={{0,4},{1,5},{2,6},{3,7},{4,0},{5,1},{6,2},{7,3},{8,12},{9,13},{10,... | collective-permute-start | bytes 589832 | tf_op jit(solution)/shard_map/ppermute | solution.py:266
  88.4 10.2 %collective-permute-start.5 = (bf16[2,24,1024]{2,1,0:T(8,128)(2,1)S(1)}, bf16[2,24,1024]{2,1,0:T(8,128)(2,1)S(1)}, u32[]{:S(2)}, u32[]{:S(2)}) collective-permute-start(bf16[2,24,1024]{2,1,0:T(8,128)(2,1)S(1)} %get-tuple-element.53), channel_id=1, source_target_pairs={{0,16},{1,17},{2,18},{3,19},{4,20},{5,21},{6,22},{7,23},{8,24},{9,... | collective-permute-start | bytes 294920 | tf_op jit(solution)/shard_map/ppermute | solution.py:266
  91.7 6.9 %collective-permute-start.6 = (bf16[2,24,1024]{2,1,0:T(8,128)(2,1)S(1)}, bf16[2,24,1024]{2,1,0:T(8,128)(2,1)S(1)}, u32[]{:S(2)}, u32[]{:S(2)}) collective-permute-start(bf16[2,24,1024]{2,1,0:T(8,128)(2,1)S(1)} %get-tuple-element.54), channel_id=1, source_target_pairs={{0,24},{1,25},{2,26},{3,27},{4,28},{5,29},{6,30},{7,31},{8,16},{9,... | collective-permute-start | bytes 294920 | tf_op jit(solution)/shard_map/ppermute | solution.py:266
  92.4 6.6 %collective-permute-start.7 = (bf16[2,24,1024]{2,1,0:T(8,128)(2,1)S(1)}, bf16[2,24,1024]{2,1,0:T(8,128)(2,1)S(1)}, u32[]{:S(2)}, u32[]{:S(2)}) collective-permute-start(bf16[2,24,1024]{2,1,0:T(8,128)(2,1)S(1)} %get-tuple-element.55), channel_id=1, source_target_pairs={{0,8},{1,9},{2,10},{3,11},{4,12},{5,13},{6,14},{7,15},{8,0},{9,1},... | collective-permute-start | bytes 294920 | tf_op jit(solution)/shard_map/ppermute | solution.py:266
